TPU v7x, 32 devices: a whole 2x2x4 slice. The times are simulated.
32 devices in a mesh: row: 4 (over z), col: 8 (over y, x, core).
Axes of the slice: x: 2, y: 2, z: 4, core: 2. Of those that a mesh axis runs over, the one named last changes fastest.
Arguments:
- query_tokens: bfloat16 [128, 32, 128], P('row'), may hold values from -14 to 14
- query_lengths: int32 [128], P('row'), may hold values from 8 to 32
- passage_tokens: bfloat16 [1024, 176, 128], P(('col', 'row')), may hold values from -8 to 8
- passage_lengths: int32 [1024], P(('col', 'row')), may hold values from 44 to 176
- student_queries: bfloat16 [128, 768], P('row', 'col'), may hold values from -28 to 28
- student_passages: bfloat16 [1024, 768], P('col', 'row'), may hold values from -0.21875 to 0.21875
- positives: int32 [128], P('row'), may hold values from 0 to 1023
Outputs:
- query_grads: float32 [128, 768], P('row', 'col')
- passage_grads: float32 [1024, 768], P('col', 'row')
- loss: float32 [], replicated
All inputs are finite; a program needn't handle non-finite values.
Results may differ from a plain program's by a relative error of at most 0.00045.
Values may be sent and summed in bfloat16 or wider, within the bound.
No kernel may reach another device: no remote copies, remote signals or barrier semaphores. Data moves between devices by JAX's collectives and lax.ppermute only.
A program may use at most 64 MiB of HBM per device.

v0:
```python
import jax
import jax.numpy as jnp
from jax import lax
from jax.sharding import PartitionSpec as P

NEG = -1e30
SCALE = 4.0


def token_block_max(query_rows, tokens, lengths):
    count = tokens.shape[1]
    result = jnp.full((query_rows.shape[0], tokens.shape[0]), NEG, jnp.float32)
    for first in range(0, count, 16):
        span = min(16, count - first)
        block = tokens[:, first : first + span, :]
        sims = jnp.einsum("ie,pte->itp", query_rows, block, preferred_element_type=jnp.float32)
        valid = (first + jnp.arange(span))[:, None] < lengths[None, :]
        sims = jnp.where(valid[None], sims, NEG)
        result = jnp.maximum(result, jnp.max(sims, axis=1))
    return result


def shards(
    query_tokens,
    query_lengths,
    passage_tokens,
    passage_lengths,
    student_queries,
    student_passages,
    positives,
):
    query_block = query_tokens.shape[0]
    slots = query_tokens.shape[1]
    width = query_tokens.shape[2]
    local_passages = passage_tokens.shape[0]
    row_count = lax.axis_size("row")
    passage_block = local_passages * row_count
    total_queries = query_block * row_count
    full_queries = lax.all_gather(student_queries, "col", axis=1, tiled=True)
    full_passages = lax.all_gather(student_passages, "row", axis=1, tiled=True)
    query_rows = query_tokens.reshape(query_block * slots, width)
    found = token_block_max(
        query_rows,
        lax.all_gather(passage_tokens, "row", axis=0, tiled=True),
        lax.all_gather(passage_lengths, "row", axis=0, tiled=True),
    )
    maxima = found
    maxima = maxima.reshape(query_block, slots, passage_block)
    query_mask = (jnp.arange(slots)[None, :] < query_lengths[:, None]).astype(jnp.float32)
    teacher = jnp.sum(maxima * query_mask[:, :, None], axis=1)
    student = SCALE * jnp.dot(full_queries, full_passages.T, preferred_element_type=jnp.float32)
    passage_start = lax.axis_index("col") * passage_block
    onehot = (passage_start + jnp.arange(passage_block))[None, :] == positives[:, None]
    positive_part = jnp.sum(jnp.where(onehot, student, 0.0), axis=1)
    local_teacher_max = jnp.max(teacher, axis=1)
    local_student_max = jnp.max(student, axis=1)
    teacher_max, student_max = lax.pmax((local_teacher_max, local_student_max), "col")
    teacher_exp = jnp.exp(teacher - teacher_max[:, None])
    student_exp = jnp.exp(student - student_max[:, None])
    teacher_sum, student_sum, cross, positive_score = lax.psum(
        (
            jnp.sum(teacher_exp, axis=1),
            jnp.sum(student_exp, axis=1),
            jnp.sum(teacher_exp * (teacher - student), axis=1),
            positive_part,
        ),
        "col",
    )
    teacher_lse = teacher_max + jnp.log(teacher_sum)
    student_lse = student_max + jnp.log(student_sum)
    per_query = cross / teacher_sum - teacher_lse + 2.0 * student_lse - positive_score
    loss = lax.psum(jnp.sum(per_query) / total_queries, "row")
    teacher_probs = teacher_exp / teacher_sum[:, None]
    student_probs = student_exp / student_sum[:, None]
    slope = (2.0 * student_probs - teacher_probs - onehot.astype(jnp.float32)) / total_queries
    query_terms = SCALE * jnp.dot(
        slope, full_passages.astype(jnp.float32), precision=lax.Precision.HIGHEST
    )
    passage_terms = SCALE * jnp.dot(
        slope.T, full_queries.astype(jnp.float32), precision=lax.Precision.HIGHEST
    )
    query_grads = lax.psum_scatter(query_terms, "col", scatter_dimension=1, tiled=True)
    passage_grads = lax.psum_scatter(passage_terms, "row", scatter_dimension=1, tiled=True)
    return (query_grads, passage_grads, loss)


def solution(mesh):
    return jax.shard_map(
        shards,
        mesh=mesh,
        in_specs=(
            P("row", None, None),
            P("row"),
            P(("col", "row"), None, None),
            P(("col", "row")),
            P("row", "col"),
            P("col", "row"),
            P("row"),
        ),
        out_specs=(P("row", "col"), P("col", "row"), P()),
        check_vma=False,
    )
```

profile of v0, /device:TPU:0, one launch (start us, length us, event | category | flops | bytes accessed | tf_op | source)
XLA Modules:
  0.0 229.6 jit_solution(14328587659485437362)
XLA Ops:
  7.2 0.0 copy-start
  7.2 0.0 all-gather.3.cloned.1.call-start
  7.2 2.9 %copy.16 = bf16[32,176,128]{2,0,1:T(8,128)(2,1)} copy(bf16[32,176,128]{2,1,0:T(8,128)(2,1)} %param.9) | data formatting | bytes 2883584 | tf_op args[2]
  10.1 0.0 all-gather.3.cloned.1.call-update
  10.1 0.0 reduce-scatter.7.cloned.1.call-start
  10.2 10.8 %all-gather = bf16[8,96,32]{1,2,0:T(8,128)(2,1)S(1)} all-gather(bf16[1,96,32]{1,2,0:T(8,128)(2,1)} %bitcast.96), channel_id=1, replica_groups=mesh['row'=4,'col'=8] {'col'}, dimensions={0}, use_global_device_ids=true | all-gather | bytes 55296 | tf_op jit(solution)/shard_map/all_gather | solution.py:39
  21.1 0.1 reshape.390
  21.2 1.2 dynamic-slice
  23.1 0.9 dynamic-update-slice
  24.0 8.6 %all-reduce = s32[128]{0:T(128)S(1)} all-reduce(s32[128]{0:T(128)S(1)} %dynamic-update-slice), channel_id=1, replica_groups=mesh['row'=4,'col'=8] {'row'}, use_global_device_ids=true, to_apply=%add | all-reduce | flops 128 | bytes 1024
  32.6 18.2 %all_gather.13 = bf16[128,768]{0,1:T(8,128)(2,1)S(1)} all-gather(bf16[128,192]{0,1:T(8,128)(2,1)} %param.12), channel_id=1, replica_groups=mesh['row'=4,'col'=8] {'row'}, dimensions={1}, use_global_device_ids=true | all-gather | bytes 245760 | tf_op jit(solution)/shard_map/all_gather | solution.py:40
  50.8 0.7 fusion.15
  51.5 0.1 iota_compare_fusion.1
  51.6 0.3 fusion.19
  51.9 71.0 %all-gather.3.cloned.1.call-done = bf16[128,176,128]{2,0,1:T(8,128)(2,1)} async-done(((bf16[32,176,128]{2,0,1:T(8,128)(2,1)}), bf16[128,176,128]{2,0,1:T(8,128)(2,1)}) %all-gather.3.cloned.1.call-update) | async-done | bytes 5767184 | tf_op jit(solution)/shard_map/all_gather | solution.py:44
  122.9 0.0 copy-done
  122.9 2.5 %fusion = f32[1024,128]{0,1:T(8,128)S(1)} fusion(pred[16,128]{1,0:T(8,128)(4,1)S(1)} %get-tuple-element.23, bf16[128,176,128]{2,0,1:T(8,128)(2,1)} %all-gather.3.cloned.1.call-done, bf16[1024,128,1]{1,0,2:T(8,128)(2,1)S(1)} %bitcast.93), kind=kOutput, calls=%fused_computation.1 | convolution fusion | flops 540934144 | bytes 6555648 | tf_op jit(solution)/shard_map/ie,pte->itp/dot_general | solution.py:16
  125.4 0.3 copy-done.2
  125.7 1.5 fusion.1
  127.2 1.5 fusion.10
  128.7 1.5 fusion.2
  130.2 1.5 fusion.3
  131.8 1.5 fusion.4
  133.3 1.5 fusion.5
  134.8 1.5 fusion.6
  136.3 1.5 fusion.7
  137.8 1.5 fusion.8
  139.4 0.0 copy-start.1
  139.4 1.5 fusion.9
  140.9 0.6 maximum_maximum_fusion
  141.5 0.2 copy.17
  141.7 0.2 multiply_reduce_fusion
  141.9 0.1 reduce_max.150
  142.0 13.8 %all-reduce.2 = (f32[32]{0:T(128)S(1)}, f32[32]{0:T(128)S(1)}) all-reduce(f32[32]{0:T(128)S(1)} %reduce_max.150, f32[32]{0:T(128)S(1)} %get-tuple-element.24), channel_id=1, replica_groups=mesh['row'=4,'col'=8] {'col'}, use_global_device_ids=true, to_apply=%region_17.18 | all-reduce | flops 64 | bytes 512 | tf_op jit(solution)/shard_map/pmax | solution.py:57
  155.9 0.0 copy-done.1
  155.9 0.2 multiply_reduce_fusion.1
  156.1 11.8 %all-reduce.1 = (f32[32]{0:T(128)S(1)}, f32[32]{0:T(128)S(1)}, f32[32]{0:T(128)S(1)}, f32[32]{0:T(128)S(1)}) all-reduce(f32[32]{0:T(128)S(1)} %get-tuple-element.4, f32[32]{0:T(128)S(1)} %get-tuple-element.6, f32[32]{0:T(128)S(1)} %get-tuple-element.5, f32[32]{0:T(128)S(1)} %get-tuple-element.3), channel_id=1, replica_groups=mesh['row'=4,'col'=8] {'col'}, use_global_device_ids=true, to_apply=%region_19.20 | all-reduce | flops 128 | bytes 1024 | tf_op jit(solution)/shard_map/psum | solution.py:60
  167.9 0.4 convolution_multiply_fusion.1
  168.3 0.9 copy.18
  169.2 0.0 reduce-scatter.7.cloned.1.call-update
  169.2 0.0 reduce-scatter.5.cloned.1.call-start
  169.2 1.2 convolution_multiply_fusion
  170.4 0.0 reduce-scatter.5.cloned.1.call-update
  170.4 0.6 subtract_reduce_fusion
  171.7 9.4 %psum.39 = f32[]{:T(128)} all-reduce(f32[]{:T(128)S(6)} %div.35), channel_id=1, replica_groups=mesh['row'=4,'col'=8] {'row'}, use_global_device_ids=true, to_apply=%region_27.28 | all-reduce | flops 1 | bytes 8 | tf_op jit(solution)/shard_map/psum | solution.py:72
  181.1 18.5 %reduce-scatter.7.cloned.1.call-done = f32[96,32]{1,0:T(8,128)} async-done(((f32[768,32]{1,0:T(8,128)}), f32[96,32]{1,0:T(8,128)}) %reduce-scatter.7.cloned.1.call-update) | async-done | bytes 12304
  199.6 1.5 copy.19
  201.1 22.0 %reduce-scatter.5.cloned.1.call-done = f32[128,192]{0,1:T(8,128)} async-done(((f32[128,768]{0,1:T(8,128)}), f32[128,192]{0,1:T(8,128)}) %reduce-scatter.5.cloned.1.call-update) | async-done | bytes 98320 | tf_op jit(solution)/shard_map/reduce_scatter | solution.py:83
  (9 shorter events, 0.1 us)
Async XLA Ops:
  7.2 115.7 %copy-start = (bf16[32,32,128]{2,1,0:T(8,128)(2,1)S(1)}, bf16[32,32,128]{2,1,0:T(8,128)(2,1)}, u32[]{:S(2)}) copy-start(bf16[32,32,128]{2,1,0:T(8,128)(2,1)} %param.7) | copy-start | bytes 786436
  7.2 115.7 %all-gather.3.cloned.1.call-start = ((), (), s32[]{:S(2)}) async-start(), calls=%async_computation.2 | async-start | bytes 7208960 | tf_op jit(solution)/shard_map/all_gather | solution.py:44
  10.1 189.5 %reduce-scatter.7.cloned.1.call-start = ((), (), s32[]{:S(2)}) async-start(), calls=%async_computation.4 | async-start | bytes 442368
  122.9 2.8 %copy-start.2 = (bf16[128,176,128]{2,0,1:T(8,128)(2,1)S(1)}, bf16[128,176,128]{2,0,1:T(8,128)(2,1)}, u32[]{:S(2)}) copy-start(bf16[128,176,128]{2,0,1:T(8,128)(2,1)} %all-gather.3.cloned.1.call-done) | copy-start | bytes 17301508
  139.4 16.5 %copy-start.1 = (s32[32]{0:T(128)S(1)}, s32[32]{0:T(128)}, u32[]{:S(2)}) copy-start(s32[32]{0:T(128)} %param.13) | copy-start | bytes 388
  169.2 53.9 %reduce-scatter.5.cloned.1.call-start = ((), (), s32[]{:S(2)}) async-start(), calls=%async_computation.3 | async-start | bytes 491520 | tf_op jit(solution)/shard_map/reduce_scatter | solution.py:83
Sparse Core Ops, SparseCore 0:
  10.3 112.5 all-gather.2
  169.3 30.2 reduce-scatter.6
  202.5 20.5 reduce-scatter.4
where the time goes:
time: 230 us
  waiting for transfers between devices  112 us (49%)
  blocking collectives  72.7 us (32%)
  matrix products  19.4 us (8%)
  between operations  15.3 us (7%)
  local copies, waits for them, and re-layouts  8.01 us (3%)
  other arithmetic  2.6 us (1%)
    all_gather x1, waiting for transfers between devices, shards(): lax.all_gather(passage_tokens, 'row', axis=0, tiled=True)  71 us
    reduce_scatter x1, waiting for transfers between devices, shards(): lax.psum_scatter(passage_terms, 'row', scatter_dimension=1, tiled=True)  22 us
    unnamed x4, waiting for transfers between devices  18.5 us
    all_gather x1, blocking collectives, shards(): full_passages = lax.all_gather(student_passages, 'row', axis=1, tiled=True)  18.2 us
    dot_general x11, matrix products, token_block_max(): jnp.einsum('ie,pte->itp', query_rows, block, preferred_element_type=jnp.f...  17.6 us
    pmax x1, blocking collectives, shards(): lax.pmax((local_teacher_max, local_student_max), 'col')  13.8 us
    psum x1, blocking collectives, shards(): lax.psum((jnp.sum(teacher_exp, axis=1), jnp.sum(student_exp, axis=1), jnp...  11.8 us
    all_gather x1, blocking collectives, shards(): full_queries = lax.all_gather(student_queries, 'col', axis=1, tiled=True)  10.8 us
  transfers between devices with their start and end apart: 3, of which 3 were waited for; matrix products, arithmetic and copies ran while one was open for 3% of the time, Pallas kernels for 0%

commit v1 on v0

v1 whole, which is shorter than its diff:
```python
import functools

import jax
import jax.numpy as jnp
from jax import lax
from jax.experimental import pallas as pl
from jax.experimental.pallas import tpu as pltpu
from jax.sharding import PartitionSpec as P

NEG = -1e30
SCALE = 4.0
VMEM_LIMIT = 56 * 1024 * 1024


def params():
    return pltpu.CompilerParams(vmem_limit_bytes=VMEM_LIMIT)


def vmem():
    return pl.BlockSpec(memory_space=pltpu.VMEM)


def smem():
    return pl.BlockSpec(memory_space=pltpu.SMEM)


def split(x, parts):
    out = []
    for _ in range(parts):
        piece = x.astype(jnp.bfloat16)
        out.append(piece)
        x = x - piece.astype(jnp.float32)
    return out


def mxu(a, b, dims=((1,), (0,))):
    return lax.dot_general(a, b, (dims, ((), ())), preferred_element_type=jnp.float32)


def teacher_kernel(offsets, slots, first, *refs):
    count = len(offsets)
    query_refs = refs[:count]
    tokens_ref, lengths_ref = refs[count : count + 2]
    rest = refs[count + 2 :]
    prior_ref = None if first else rest[0]
    out_ref, best = rest[-2:]
    passages, span, width = tokens_ref.shape
    queries = out_ref.shape[1]
    r, c = lax.axis_index("row"), lax.axis_index("col")
    total = jnp.zeros(out_ref.shape, jnp.float32) if first else prior_ref[...]
    for query_ref, offset in zip(query_refs, offsets):
        rows = query_ref.shape[0]
        tile = min(256, rows)

        def passage(p, carry, query_ref=query_ref, rows=rows, tile=tile):
            block = tokens_ref[p]
            live = lax.broadcasted_iota(jnp.int32, (span, tile), 0) < lengths_ref[p]
            for n in range(0, rows, tile):
                sims = mxu(block, query_ref[n : n + tile, :], ((1,), (1,)))
                sims = jnp.where(live, sims, NEG)
                best[pl.ds(p, 1), n : n + tile] = jnp.max(sims, axis=0, keepdims=True)
            return carry

        lax.fori_loop(0, passages, passage, 0)
        start = offset(r, c)
        owner = lax.broadcasted_iota(jnp.int32, (rows, queries), 0) // slots + start
        member = (owner == lax.broadcasted_iota(jnp.int32, (rows, queries), 1)).astype(jnp.bfloat16)
        for piece in split(best[:, :rows], 3):
            total = total + mxu(piece, member)
    out_ref[...] = total


def teacher_block(blocks, offsets, slots, tokens, lengths, prior, queries):
    passages = tokens.shape[0]
    operands = list(blocks) + [tokens, lengths]
    specs = [vmem()] * len(blocks) + [vmem(), smem()]
    if prior is not None:
        operands.append(prior)
        specs.append(vmem())
    rows = max(b.shape[0] for b in blocks)
    flops = 2 * sum(b.shape[0] for b in blocks) * tokens.size
    return pl.pallas_call(
        functools.partial(teacher_kernel, offsets, slots, prior is None),
        out_shape=jax.ShapeDtypeStruct((passages, queries), jnp.float32),
        in_specs=specs,
        out_specs=vmem(),
        scratch_shapes=[pltpu.VMEM((passages, rows), jnp.float32)],
        compiler_params=params(),
        cost_estimate=pl.CostEstimate(flops=flops, bytes_accessed=2 * tokens.size, transcendentals=0),
    )(*operands)


def student_kernel(R, C, *refs):
    sq_refs = refs[:C]
    sp_refs = refs[C : C + R]
    score_ref, vectors_ref, pos_ref, held = refs[C + R :]
    per = C // R
    r, c = lax.axis_index("row"), lax.axis_index("col")
    block = sq_refs[0].shape[1]
    wide = sp_refs[0].shape[0] // per
    queries = R * block
    for kc in range(C):
        for kr in range(R):
            held[c ^ kc, r ^ kr] = sq_refs[kc][kr]
    total = jnp.zeros((queries, sp_refs[0].shape[1]), jnp.float32)
    for k in range(R):
        pieces = [
            held[(r ^ k) * per + h].reshape(queries, held.shape[3]).astype(jnp.float32)[:, :wide] for h in range(per)
        ]
        vectors = jnp.concatenate(pieces, axis=1).astype(jnp.bfloat16)
        if k == 0:
            vectors_ref[...] = vectors
        total = total + mxu(vectors, sp_refs[k][...])
    score_ref[...] = (SCALE * total).T
    meta = held[c].reshape(queries, held.shape[3]).astype(jnp.float32)
    where = meta[:, wide : wide + 1] * 64.0 + meta[:, wide + 1 : wide + 2]
    diag = lax.broadcasted_iota(jnp.int32, (queries, queries), 0) == lax.broadcasted_iota(
        jnp.int32, (queries, queries), 1
    )
    pos_ref[...] = jnp.sum(jnp.where(diag, where, 0.0), axis=0, keepdims=True)


def student_scores(sq, sp, R, C):
    block, lanes = sq[0].shape[1:]
    queries, depth, passages = R * block, sp[0].shape[0], sp[0].shape[1]
    return pl.pallas_call(
        functools.partial(student_kernel, R, C),
        out_shape=(
            jax.ShapeDtypeStruct((passages, queries), jnp.float32),
            jax.ShapeDtypeStruct((queries, depth), jnp.bfloat16),
            jax.ShapeDtypeStruct((1, queries), jnp.float32),
        ),
        in_specs=[vmem()] * (C + R),
        out_specs=(vmem(),) * 3,
        scratch_shapes=[pltpu.VMEM((C, R, block, lanes), jnp.bfloat16)],
        compiler_params=params(),
    )(*sq, *sp)


def finish_kernel(R, C, block, *refs):
    t_refs, s_refs, d_refs = refs[:C], refs[C : 2 * C], refs[2 * C : 3 * C]
    vectors_ref, pos_ref, query_ref, passage_ref, loss_ref, teach, stud = refs[3 * C :]
    r, c = lax.axis_index("row"), lax.axis_index("col")
    per = C // R
    queries = pos_ref.shape[1]
    wide = d_refs[0].shape[0]
    span = s_refs[0].shape[0]
    shape = (span, queries)
    for kc in range(C):
        for kr in range(R):
            teach[c ^ kc, r ^ kr] = t_refs[kc][kr]
        stud[c ^ kc] = s_refs[kc][...]

    def rows(op, x):
        return op(x, axis=0, keepdims=True)

    def peak(i, carry):
        t_max, s_max = carry
        return jnp.maximum(t_max, teach[i].reshape(shape)), jnp.maximum(s_max, stud[i])

    low = jnp.full(shape, -jnp.inf, jnp.float32)
    t_max, s_max = lax.fori_loop(0, C, peak, (low, low))
    t_max, s_max = rows(jnp.max, t_max), rows(jnp.max, s_max)
    place = pos_ref[...].astype(jnp.int32)
    index = lax.broadcasted_iota(jnp.int32, shape, 0)

    def totals(i, carry):
        t_sum, s_sum, cross, score = carry
        t, s = teach[i].reshape(shape), stud[i]
        t_exp, s_exp = jnp.exp(t - t_max), jnp.exp(s - s_max)
        hot = index + i * span == place
        teach[i] = t_exp.reshape(R, span // R, queries)
        stud[i] = s_exp
        return (
            t_sum + rows(jnp.sum, t_exp),
            s_sum + rows(jnp.sum, s_exp),
            cross + rows(jnp.sum, t_exp * (t - s)),
            score + rows(jnp.sum, jnp.where(hot, s, 0.0)),
        )

    zero = jnp.zeros((1, queries), jnp.float32)
    t_sum, s_sum, cross, score = lax.fori_loop(0, C, totals, (zero,) * 4)
    t_lse = t_max + jnp.log(t_sum)
    s_lse = s_max + jnp.log(s_sum)
    each = cross / t_sum - t_lse + 2.0 * s_lse - score
    loss_ref[...] = jnp.sum(each, axis=1, keepdims=True) / queries
    factor = SCALE / queries
    t_factor, s_factor = factor / t_sum, 2.0 * factor / s_sum

    def slope(i):
        hot = index + i * span == place
        gap = stud[i] * s_factor - teach[i].reshape(shape) * t_factor
        return split(gap - jnp.where(hot, factor, 0.0), 2)

    total = jnp.zeros((wide, queries), jnp.float32)
    group = r * per + c % per
    for k in range(C):
        for piece in slope(group ^ k):
            total = total + mxu(d_refs[k][...], piece)
    flat = total.T
    query_ref[...] = functools.reduce(
        jnp.add, [jnp.where(r == i, flat[i * block : (i + 1) * block, :], 0.0) for i in range(R)]
    )
    grads = sum(mxu(piece, vectors_ref[...]) for piece in slope(c))
    passage_ref[...] = grads.T


def finish(t, s, d, vectors, pos, R, C, block):
    queries = pos.shape[1]
    span = s[0].shape[0]
    return pl.pallas_call(
        functools.partial(finish_kernel, R, C, block),
        out_shape=(
            jax.ShapeDtypeStruct((block, d[0].shape[0]), jnp.float32),
            jax.ShapeDtypeStruct((vectors.shape[1], span), jnp.float32),
            jax.ShapeDtypeStruct((1, 1), jnp.float32),
        ),
        in_specs=[vmem()] * (3 * C + 2),
        out_specs=(vmem(),) * 3,
        scratch_shapes=[
            pltpu.VMEM((C, R, span // R, queries), jnp.float32),
            pltpu.VMEM((C, span, queries), jnp.float32),
        ],
        compiler_params=params(),
    )(*t, *s, *d, vectors, pos)


def shards(query_tokens, query_lengths, passage_tokens, passage_lengths, student_queries, student_passages, positives):
    R, C = lax.axis_size("row"), lax.axis_size("col")
    r, c = lax.axis_index("row"), lax.axis_index("col")
    block, slots, width = query_tokens.shape
    queries = block * R
    local = passage_tokens.shape[0]
    per = C // R

    def over_row(x, k):
        return lax.ppermute(x, "row", [(i, i ^ k) for i in range(R)])

    def over_col(x, k):
        return lax.ppermute(x, "col", [(i, i ^ k) for i in range(C)])

    live = jnp.arange(slots)[None, :] < query_lengths[:, None]
    tokens = jnp.where(live[:, :, None], query_tokens, 0).reshape(block * slots, width)
    half = block // 2
    mine = lax.dynamic_slice_in_dim(tokens, (c % 2) * half * slots, half * slots, 0)
    near = [over_row(mine, k) for k in range(1, R)]
    far = [over_col(x, 1) for x in near]

    wide = student_queries.shape[1]
    meta = jnp.stack([positives // 64, positives % 64], axis=1).astype(jnp.bfloat16)
    sent = jnp.pad(jnp.concatenate([student_queries, meta], axis=1), ((0, 0), (0, -(wide + 2) % 128)))
    sq_row = jnp.stack([sent] + [over_row(sent, k) for k in range(1, R)])
    sq = [sq_row] + [over_col(sq_row, k) for k in range(1, C)]
    flipped = student_passages.T
    sp = [flipped] + [over_row(flipped, k) for k in range(1, R)]
    parts = flipped.reshape(per, flipped.shape[0] // per, flipped.shape[1])
    chosen = [lax.dynamic_index_in_dim(parts, (c % per) ^ j, 0, keepdims=False) for j in range(per)]
    d = []
    for k in range(C):
        pairs = []
        for row in range(R):
            for col in range(C):
                group = col ^ k
                pairs.append((row * C + col, (group // per) * C + row * per + group % per))
        d.append(lax.ppermute(chosen[k % per], ("row", "col"), pairs))

    score = teacher_block(
        [tokens], [lambda r, c: r * block], slots, passage_tokens, passage_lengths, None, queries
    )
    own, vectors, pos = student_scores(sq, sp, R, C)

    def spread(x):
        pieces, bit = [x], C // 2
        while bit:
            pieces = pieces + [over_col(p, bit) for p in pieces]
            bit //= 2
        order, bit = [0], C // 2
        while bit:
            order = order + [o ^ bit for o in order]
            bit //= 2
        return [pieces[order.index(k)] for k in range(C)]

    s = spread(own)
    for k in range(1, R):
        offsets = [
            lambda r, c, k=k: (r ^ k) * block + (c % 2) * half,
            lambda r, c, k=k: (r ^ k) * block + (1 - c % 2) * half,
        ]
        score = teacher_block(
            [near[k - 1], far[k - 1]], offsets, slots, passage_tokens, passage_lengths, score, queries
        )
    stacked = jnp.stack([score] + [over_row(score, k) for k in range(1, R)])
    t = spread(stacked)
    query_grads, passage_grads, loss = finish(t, s, d, vectors, pos, R, C, block)
    return (query_grads, passage_grads.T, loss[0, 0])


def solution(mesh):
    return jax.shard_map(
        shards,
        mesh=mesh,
        in_specs=(
            P("row", None, None),
            P("row"),
            P(("col", "row"), None, None),
            P(("col", "row")),
            P("row", "col"),
            P("col", "row"),
            P("row"),
        ),
        out_specs=(P("row", "col"), P("col", "row"), P()),
        check_vma=False,
    )
```

time: 230 us -> 138 us (0.60)
  the two profiles are of different devices: /device:TPU:0 before, /device:TPU:5 now
where the time goes in v1:
time: 138 us; the launch traced here: 137 us
  Pallas kernels  66.2 us (48%)
  starting transfers between devices  59.5 us (43%)
  other arithmetic  4.14 us (3%)
  waiting for transfers between devices  3.75 us (3%)
  local copies, waits for them, and re-layouts  2.75 us (2%)
    pallas_call x4, Pallas kernels, teacher_block(): pl.pallas_call(functools.partial(teacher_kernel, offsets, slots, prior is...  61.1 us
    ppermute x24, starting transfers between devices, over_col(): return lax.ppermute(x, 'col', [(i, i ^ k) for i in range(C)])  24.5 us
    ppermute x8, starting transfers between devices, shards(): d.append(lax.ppermute(chosen[k % per], ('row', 'col'), pairs))  20.5 us
    ppermute x12, starting transfers between devices, over_row(): return lax.ppermute(x, 'row', [(i, i ^ k) for i in range(R)])  14.5 us
    pallas_call x1, Pallas kernels, finish(): pl.pallas_call(functools.partial(finish_kernel, R, C, block), out_shape=(...  3.05 us
  transfers between devices with their start and end apart: 44, of which 4 were waited for; matrix products, arithmetic and copies ran while one was open for 3% of the time, Pallas kernels for 46%

profile of v1, /device:TPU:5, one launch (start us, length us, event | category | flops | bytes accessed | tf_op | source)
XLA Modules:
  0.0 137.4 jit_solution(7179838630912720062)
XLA Ops:
  0.6 0.7 convert_bitcast_fusion
  1.5 0.8 fusion.4
  2.3 1.3 collective-permute-start.16
  3.6 2.3 %collective-permute-start.17 = (bf16[32,128]{1,0:T(8,128)(2,1)S(1)}, bf16[32,128]{1,0:T(8,128)(2,1)S(1)}, u32[]{:S(2)}, u32[]{:S(2)}) collective-permute-start(bf16[32,128]{1,0:T(8,128)(2,1)S(1)} %fusion.4), channel_id=1, source_target_pairs={{0,16},{8,24},{16,0},{24,8},{1,17},{9,25},{17,1},{25,9},{2,18},{10... | collective-permute-start | bytes 24584 | tf_op jit(solution)/shard_map/ppermute | solution.py:237
  5.9 0.7 iota_compare_fusion.1
  6.6 1.2 broadcast_select_fusion
  8.2 3.2 %collective-permute-start.2 = (bf16[512,128]{1,0:T(8,128)(2,1)S(1)}, bf16[512,128]{1,0:T(8,128)(2,1)S(1)}, u32[]{:S(2)}, u32[]{:S(2)}) collective-permute-start(bf16[512,128]{1,0:T(8,128)(2,1)S(1)} %constant_dynamic-slice_fusion), channel_id=1, source_target_pairs={{0,16},{8,24},{16,0},{24,8},{1,17},{9,25},{17,1},{25,9},{2,18},{10... | collective-permute-start | bytes 393224 | tf_op jit(solution)/shard_map/ppermute | solution.py:237
  11.4 0.8 dynamic-slice_bitcast_fusion
  12.2 11.1 %shard_map.94.refs_4_ = f32[32,128]{1,0:T(8,128)} custom-call(bf16[1024,128]{1,0:T(8,128)(2,1)} %bitcast.24, bf16[32,176,128]{2,1,0:T(8,128)(2,1)} %refs_2_.7, s32[32]{0:T(128)} %refs_3_.5), custom_call_target="tpu_custom_call" | custom-call | flops 1476395008 | bytes 1441792 | tf_op jit(solution)/shard_map/pallas_call | solution.py:82
  23.3 2.1 %collective-permute-start.5 = (bf16[512,128]{1,0:T(8,128)(2,1)S(1)}, bf16[512,128]{1,0:T(8,128)(2,1)S(1)}, u32[]{:S(2)}, u32[]{:S(2)}) collective-permute-start(bf16[512,128]{1,0:T(8,128)(2,1)S(1)} %collective-permute-done.4.refs_0_), channel_id=1, source_target_pairs={{0,1},{1,0},{2,3},{3,2},{4,5},{5,4},{6,7},{7,6},{8,9},{9,8},{10,11... | collective-permute-start | bytes 393224 | tf_op jit(solution)/shard_map/ppermute | solution.py:240
  25.5 1.3 collective-permute-start.25
  26.8 1.2 collective-permute-start.24
  28.1 0.7 collective-permute-start.23
  28.8 0.6 copy-done.40
  29.4 16.7 %shard_map.95.refs_4_ = f32[32,128]{1,0:T(8,128)} custom-call(bf16[512,128]{1,0:T(8,128)(2,1)} %copy-done.39, bf16[512,128]{1,0:T(8,128)(2,1)} %copy-done.40, bf16[32,176,128]{2,1,0:T(8,128)(2,1)} %refs_2_.7, s32[32]{0:T(128)} %refs_3_.5, f32[32,128]{1,0:T(8,128)} %shard_map.94.refs_4_), custom_call_target="tpu_custom_call" | custom-call | flops 1476395008 | bytes 1441792 | tf_op jit(solution)/shard_map/pallas_call | solution.py:82
  46.1 1.3 collective-permute-start.22
  47.4 1.3 collective-permute-start.21
  49.0 0.6 collective-permute-start.19
  49.7 0.6 copy-done.41
  50.3 16.7 %shard_map.96.refs_4_ = f32[32,128]{1,0:T(8,128)} custom-call(bf16[512,128]{1,0:T(8,128)(2,1)} %copy-done.37, bf16[512,128]{1,0:T(8,128)(2,1)} %copy-done.41, bf16[32,176,128]{2,1,0:T(8,128)(2,1)} %refs_2_.7, s32[32]{0:T(128)} %refs_3_.5, f32[32,128]{1,0:T(8,128)} %shard_map.95.refs_4_), custom_call_target="tpu_custom_call" | custom-call | flops 1476395008 | bytes 1441792 | tf_op jit(solution)/shard_map/pallas_call | solution.py:82
  67.1 3.7 %collective-permute-start.41 = (bf16[96,128]{1,0:T(8,128)(2,1)S(1)}, bf16[96,128]{1,0:T(8,128)(2,1)S(1)}, u32[]{:S(2)}, u32[]{:S(2)}) collective-permute-start(bf16[96,128]{1,0:T(8,128)(2,1)S(1)} %get-tuple-element.15), channel_id=1, source_target_pairs={{0,17},{1,16},{2,25},{3,24},{4,1},{5,0},{6,9},{7,8},{8,19},{9,18},... | collective-permute-start | bytes 73736 | tf_op jit(solution)/shard_map/ppermute | solution.py:265
  70.8 1.0 collective-permute-start.28
  71.9 2.6 %collective-permute-start.26 = (bf16[192,128]{1,0:T(8,128)(2,1)S(1)}, bf16[192,128]{1,0:T(8,128)(2,1)S(1)}, u32[]{:S(2)}, u32[]{:S(2)}) collective-permute-start(bf16[192,128]{1,0:T(8,128)(2,1)S(1)} %bitcast.29), channel_id=1, source_target_pairs={{0,8},{8,0},{16,24},{24,16},{1,9},{9,1},{17,25},{25,17},{2,10},{10... | collective-permute-start | bytes 147464 | tf_op jit(solution)/shard_map/ppermute | solution.py:237
  74.5 16.7 %shard_map.97 = f32[32,128]{1,0:T(8,128)} custom-call(bf16[512,128]{1,0:T(8,128)(2,1)} %copy-done.38, bf16[512,128]{1,0:T(8,128)(2,1)} %copy-done.42, bf16[32,176,128]{2,1,0:T(8,128)(2,1)} %refs_2_.7, s32[32]{0:T(128)} %refs_3_.5, f32[32,128]{1,0:T(8,128)} %shard_map.96.refs_4_), custom_call_target="tpu_custom_call" | custom-call | flops 1476395008 | bytes 1441792 | tf_op jit(solution)/shard_map/pallas_call | solution.py:82
  91.2 1.0 collective-permute-start.8
  92.2 0.9 collective-permute-start.7
  93.1 1.7 %collective-permute-start.6 = (f32[32,128]{1,0:T(8,128)}, f32[32,128]{1,0:T(8,128)S(1)}, u32[]{:S(2)}, u32[]{:S(2)}) collective-permute-start(f32[32,128]{1,0:T(8,128)} %shard_map.97), channel_id=1, source_target_pairs={{0,8},{8,0},{16,24},{24,16},{1,9},{9,1},{17,25},{25,17},{2,10},{10... | collective-permute-start | bytes 49160 | tf_op jit(solution)/shard_map/ppermute | solution.py:237
  94.8 2.0 %shard_map.98 = (f32[128,128]{1,0:T(8,128)}, bf16[128,192]{1,0:T(8,128)(2,1)}, f32[1,128]{1,0:T(1,128)}) custom-call(bf16[4,32,128]{2,1,0:T(8,128)(2,1)} %copy-done.3, bf16[4,32,128]{2,1,0:T(8,128)(2,1)} %copy-done.27, bf16[4,32,128]{2,1,0:T(8,128)(2,1)} %copy-done.26, bf16[4,32,128]{2,1,0:T(8,128)(2,1)} %copy-done.25, bf16[4,32,128]{2,1,0:T(8,128)(2,1)} %copy-done.24, ...), custom_call_target="tpu_custom_call" | custom-call | tf_op jit(solution)/shard_map/pallas_call | solution.py:126
  96.9 3.7 %collective-permute-start.39 = (bf16[96,128]{1,0:T(8,128)(2,1)S(1)}, bf16[96,128]{1,0:T(8,128)(2,1)S(1)}, u32[]{:S(2)}, u32[]{:S(2)}) collective-permute-start(bf16[96,128]{1,0:T(8,128)(2,1)S(1)} %get-tuple-element.15), channel_id=1, source_target_pairs={{0,9},{1,8},{2,1},{3,0},{4,25},{5,24},{6,17},{7,16},{8,11},{9,10},... | collective-permute-start | bytes 73736 | tf_op jit(solution)/shard_map/ppermute | solution.py:265
  100.5 2.3 %collective-permute-start.42 = (bf16[96,128]{1,0:T(8,128)(2,1)S(1)}, bf16[96,128]{1,0:T(8,128)(2,1)S(1)}, u32[]{:S(2)}, u32[]{:S(2)}) collective-permute-start(bf16[96,128]{1,0:T(8,128)(2,1)S(1)} %get-tuple-element.16), channel_id=1, source_target_pairs={{0,24},{1,25},{2,16},{3,17},{4,8},{5,9},{6,0},{7,1},{8,26},{9,27},... | collective-permute-start | bytes 73736 | tf_op jit(solution)/shard_map/ppermute | solution.py:265
  102.9 2.0 %collective-permute-start.40 = (bf16[96,128]{1,0:T(8,128)(2,1)S(1)}, bf16[96,128]{1,0:T(8,128)(2,1)S(1)}, u32[]{:S(2)}, u32[]{:S(2)}) collective-permute-start(bf16[96,128]{1,0:T(8,128)(2,1)S(1)} %get-tuple-element.16), channel_id=1, source_target_pairs={{0,16},{1,17},{2,24},{3,25},{4,0},{5,1},{6,8},{7,9},{8,18},{9,19},... | collective-permute-start | bytes 73736 | tf_op jit(solution)/shard_map/ppermute | solution.py:265
  104.9 0.7 pad_maximum_fusion.refs_0_
  105.7 1.2 collective-permute-start.30
  106.9 1.4 %collective-permute-start.29 = (f32[128,128]{1,0:T(8,128)}, f32[128,128]{1,0:T(8,128)S(1)}, u32[]{:S(2)}, u32[]{:S(2)}) collective-permute-start(f32[128,128]{1,0:T(8,128)} %get-tuple-element.9.refs_8_), channel_id=1, source_target_pairs={{0,1},{1,0},{2,3},{3,2},{4,5},{5,4},{6,7},{7,6},{8,9},{9,8},{10,11... | collective-permute-start | bytes 196616 | tf_op jit(solution)/shard_map/ppermute | solution.py:240
  108.3 1.3 collective-permute-start.12
  109.7 3.4 %collective-permute-start.38 = (bf16[96,128]{1,0:T(8,128)(2,1)S(1)}, bf16[96,128]{1,0:T(8,128)(2,1)S(1)}, u32[]{:S(2)}, u32[]{:S(2)}) collective-permute-start(bf16[96,128]{1,0:T(8,128)(2,1)S(1)} %get-tuple-element.16), channel_id=1, source_target_pairs={{0,8},{1,9},{2,0},{3,1},{4,24},{5,25},{6,16},{7,17},{8,10},{9,11},... | collective-permute-start | bytes 73736 | tf_op jit(solution)/shard_map/ppermute | solution.py:265
  113.1 1.9 %collective-permute-done.38.refs_18_ = bf16[96,128]{1,0:T(8,128)(2,1)S(1)} collective-permute-done((bf16[96,128]{1,0:T(8,128)(2,1)S(1)}, bf16[96,128]{1,0:T(8,128)(2,1)S(1)}, u32[]{:S(2)}, u32[]{:S(2)}) %collective-permute-start.38) | collective-permute-done | bytes 24608 | tf_op jit(solution)/shard_map/ppermute | solution.py:265
  115.0 5.3 %collective-permute-start.36 = (bf16[96,128]{1,0:T(8,128)(2,1)S(1)}, bf16[96,128]{1,0:T(8,128)(2,1)S(1)}, u32[]{:S(2)}, u32[]{:S(2)}) collective-permute-start(bf16[96,128]{1,0:T(8,128)(2,1)S(1)} %get-tuple-element.16), channel_id=1, source_target_pairs={{0,0},{1,1},{2,8},{3,9},{4,16},{5,17},{6,24},{7,25},{8,2},{9,3},{1... | collective-permute-start | bytes 73736 | tf_op jit(solution)/shard_map/ppermute | solution.py:265
  120.3 1.3 collective-permute-start.34
  121.6 2.4 %collective-permute-start.33 = (f32[128,128]{1,0:T(8,128)S(1)}, f32[128,128]{1,0:T(8,128)S(1)}, u32[]{:S(2)}, u32[]{:S(2)}) collective-permute-start(f32[128,128]{1,0:T(8,128)S(1)} %collective-permute-done.32.refs_12_), channel_id=1, source_target_pairs={{0,1},{1,0},{2,3},{3,2},{4,5},{5,4},{6,7},{7,6},{8,9},{9,8},{10,11... | collective-permute-start | bytes 196616 | tf_op jit(solution)/shard_map/ppermute | solution.py:240
  124.1 3.7 %collective-permute-start.10 = (f32[4,32,128]{2,1,0:T(8,128)S(1)}, f32[4,32,128]{2,1,0:T(8,128)S(1)}, u32[]{:S(2)}, u32[]{:S(2)}) collective-permute-start(f32[4,32,128]{2,1,0:T(8,128)S(1)} %pad_maximum_fusion.refs_0_), channel_id=1, source_target_pairs={{0,2},{1,3},{2,0},{3,1},{4,6},{5,7},{6,4},{7,5},{8,10},{9,11},{10,... | collective-permute-start | bytes 196616 | tf_op jit(solution)/shard_map/ppermute | solution.py:240
  127.9 0.7 collective-permute-start.35
  129.2 0.8 collective-permute-done.10.refs_2_
  129.9 0.9 collective-permute-start.11
  131.0 1.9 %collective-permute-start.15 = (f32[4,32,128]{2,1,0:T(8,128)S(1)}, f32[4,32,128]{2,1,0:T(8,128)S(1)}, u32[]{:S(2)}, u32[]{:S(2)}) collective-permute-start(f32[4,32,128]{2,1,0:T(8,128)S(1)} %collective-permute-done.14.refs_6_), channel_id=1, source_target_pairs={{0,1},{1,0},{2,3},{3,2},{4,5},{5,4},{6,7},{7,6},{8,9},{9,8},{10,11... | collective-permute-start | bytes 196616 | tf_op jit(solution)/shard_map/ppermute | solution.py:240
  132.9 0.8 collective-permute-done.15.refs_7_
  133.9 0.4 copy-done.17
  134.3 3.0 %shard_map.99 = (f32[32,96]{1,0:T(8,128)}, f32[192,128]{1,0:T(8,128)}, f32[1,1]{1,0:T(1,128)}) custom-call(f32[4,32,128]{2,1,0:T(8,128)} %copy-done.1, f32[4,32,128]{2,1,0:T(8,128)} %copy-done.14, f32[4,32,128]{2,1,0:T(8,128)} %copy-done.11, f32[4,32,128]{2,1,0:T(8,128)} %copy-done.16, f32[4,32,128]{2,1,0:T(8,128)} %copy-done.7, f32[4,32,128]{2,1,0:T(8,128)} %copy-done.15, ...), custom_call_target="tpu_custom_call" | custom-call | tf_op jit(solution)/shard_map/pallas_call | solution.py:211
  (143 shorter events, 2.3 us)
Async XLA Ops:
  2.3 23.1 %collective-permute-start.16 = (bf16[32,128]{1,0:T(8,128)(2,1)S(1)}, bf16[32,128]{1,0:T(8,128)(2,1)S(1)}, u32[]{:S(2)}, u32[]{:S(2)}) collective-permute-start(bf16[32,128]{1,0:T(8,128)(2,1)S(1)} %fusion.4), channel_id=1, source_target_pairs={{0,8},{8,0},{16,24},{24,16},{1,9},{9,1},{17,25},{25,17},{2,10},{10... | collective-permute-start | bytes 24584 | tf_op jit(solution)/shard_map/ppermute | solution.py:237
  3.6 21.9 %collective-permute-start.17 = (bf16[32,128]{1,0:T(8,128)(2,1)S(1)}, bf16[32,128]{1,0:T(8,128)(2,1)S(1)}, u32[]{:S(2)}, u32[]{:S(2)}) collective-permute-start(bf16[32,128]{1,0:T(8,128)(2,1)S(1)} %fusion.4), channel_id=1, source_target_pairs={{0,16},{8,24},{16,0},{24,8},{1,17},{9,25},{17,1},{25,9},{2,18},{10... | collective-permute-start | bytes 24584 | tf_op jit(solution)/shard_map/ppermute | solution.py:237
  5.9 19.6 %collective-permute-start.18 = (bf16[32,128]{1,0:T(8,128)(2,1)S(1)}, bf16[32,128]{1,0:T(8,128)(2,1)S(1)}, u32[]{:S(2)}, u32[]{:S(2)}) collective-permute-start(bf16[32,128]{1,0:T(8,128)(2,1)S(1)} %fusion.4), channel_id=1, source_target_pairs={{0,24},{8,16},{16,8},{24,0},{1,25},{9,17},{17,9},{25,1},{2,26},{10... | collective-permute-start | bytes 24584 | tf_op jit(solution)/shard_map/ppermute | solution.py:237
  7.8 15.4 %collective-permute-start.4 = (bf16[512,128]{1,0:T(8,128)(2,1)S(1)}, bf16[512,128]{1,0:T(8,128)(2,1)S(1)}, u32[]{:S(2)}, u32[]{:S(2)}) collective-permute-start(bf16[512,128]{1,0:T(8,128)(2,1)S(1)} %constant_dynamic-slice_fusion), channel_id=1, source_target_pairs={{0,8},{8,0},{16,24},{24,16},{1,9},{9,1},{17,25},{25,17},{2,10},{10... | collective-permute-start | bytes 393224 | tf_op jit(solution)/shard_map/ppermute | solution.py:237
  8.2 19.8 %collective-permute-start.2 = (bf16[512,128]{1,0:T(8,128)(2,1)S(1)}, bf16[512,128]{1,0:T(8,128)(2,1)S(1)}, u32[]{:S(2)}, u32[]{:S(2)}) collective-permute-start(bf16[512,128]{1,0:T(8,128)(2,1)S(1)} %constant_dynamic-slice_fusion), channel_id=1, source_target_pairs={{0,16},{8,24},{16,0},{24,8},{1,17},{9,25},{17,1},{25,9},{2,18},{10... | collective-permute-start | bytes 393224 | tf_op jit(solution)/shard_map/ppermute | solution.py:237
  23.3 5.5 %collective-permute-start.5 = (bf16[512,128]{1,0:T(8,128)(2,1)S(1)}, bf16[512,128]{1,0:T(8,128)(2,1)S(1)}, u32[]{:S(2)}, u32[]{:S(2)}) collective-permute-start(bf16[512,128]{1,0:T(8,128)(2,1)S(1)} %collective-permute-done.4.refs_0_), channel_id=1, source_target_pairs={{0,1},{1,0},{2,3},{3,2},{4,5},{5,4},{6,7},{7,6},{8,9},{9,8},{10,11... | collective-permute-start | bytes 393224 | tf_op jit(solution)/shard_map/ppermute | solution.py:240
  25.4 23.6 %collective-permute-start = (bf16[512,128]{1,0:T(8,128)(2,1)S(1)}, bf16[512,128]{1,0:T(8,128)(2,1)S(1)}, u32[]{:S(2)}, u32[]{:S(2)}) collective-permute-start(bf16[512,128]{1,0:T(8,128)(2,1)S(1)} %constant_dynamic-slice_fusion), channel_id=1, source_target_pairs={{0,24},{8,16},{16,8},{24,0},{1,25},{9,17},{17,9},{25,1},{2,26},{10... | collective-permute-start | bytes 393224 | tf_op jit(solution)/shard_map/ppermute | solution.py:237
  25.5 20.6 %collective-permute-start.25 = (bf16[4,32,128]{2,1,0:T(8,128)(2,1)S(1)}, bf16[4,32,128]{2,1,0:T(8,128)(2,1)S(1)}, u32[]{:S(2)}, u32[]{:S(2)}) collective-permute-start(bf16[4,32,128]{2,1,0:T(8,128)(2,1)S(1)} %pad_maximum_fusion.1.refs_0_), channel_id=1, source_target_pairs={{0,7},{1,6},{2,5},{3,4},{4,3},{5,2},{6,1},{7,0},{8,15},{9,14},{10,... | collective-permute-start | bytes 98312 | tf_op jit(solution)/shard_map/ppermute | solution.py:240
  26.8 20.6 %collective-permute-start.24 = (bf16[4,32,128]{2,1,0:T(8,128)(2,1)S(1)}, bf16[4,32,128]{2,1,0:T(8,128)(2,1)S(1)}, u32[]{:S(2)}, u32[]{:S(2)}) collective-permute-start(bf16[4,32,128]{2,1,0:T(8,128)(2,1)S(1)} %pad_maximum_fusion.1.refs_0_), channel_id=1, source_target_pairs={{0,6},{1,7},{2,4},{3,5},{4,2},{5,3},{6,0},{7,1},{8,14},{9,15},{10,... | collective-permute-start | bytes 98312 | tf_op jit(solution)/shard_map/ppermute | solution.py:240
  28.1 20.7 %collective-permute-start.23 = (bf16[4,32,128]{2,1,0:T(8,128)(2,1)S(1)}, bf16[4,32,128]{2,1,0:T(8,128)(2,1)S(1)}, u32[]{:S(2)}, u32[]{:S(2)}) collective-permute-start(bf16[4,32,128]{2,1,0:T(8,128)(2,1)S(1)} %pad_maximum_fusion.1.refs_0_), channel_id=1, source_target_pairs={{0,5},{1,4},{2,7},{3,6},{4,1},{5,0},{6,3},{7,2},{8,13},{9,12},{10,... | collective-permute-start | bytes 98312 | tf_op jit(solution)/shard_map/ppermute | solution.py:240
  28.8 20.9 %collective-permute-start.3 = (bf16[512,128]{1,0:T(8,128)(2,1)S(1)}, bf16[512,128]{1,0:T(8,128)(2,1)S(1)}, u32[]{:S(2)}, u32[]{:S(2)}) collective-permute-start(bf16[512,128]{1,0:T(8,128)(2,1)S(1)} %collective-permute-done.2.refs_0_), channel_id=1, source_target_pairs={{0,1},{1,0},{2,3},{3,2},{4,5},{5,4},{6,7},{7,6},{8,9},{9,8},{10,11... | collective-permute-start | bytes 393224 | tf_op jit(solution)/shard_map/ppermute | solution.py:240
  46.1 20.9 %collective-permute-start.22 = (bf16[4,32,128]{2,1,0:T(8,128)(2,1)S(1)}, bf16[4,32,128]{2,1,0:T(8,128)(2,1)S(1)}, u32[]{:S(2)}, u32[]{:S(2)}) collective-permute-start(bf16[4,32,128]{2,1,0:T(8,128)(2,1)S(1)} %pad_maximum_fusion.1.refs_0_), channel_id=1, source_target_pairs={{0,4},{1,5},{2,6},{3,7},{4,0},{5,1},{6,2},{7,3},{8,12},{9,13},{10,... | collective-permute-start | bytes 98312 | tf_op jit(solution)/shard_map/ppermute | solution.py:240
  47.4 19.7 %collective-permute-start.21 = (bf16[4,32,128]{2,1,0:T(8,128)(2,1)S(1)}, bf16[4,32,128]{2,1,0:T(8,128)(2,1)S(1)}, u32[]{:S(2)}, u32[]{:S(2)}) collective-permute-start(bf16[4,32,128]{2,1,0:T(8,128)(2,1)S(1)} %pad_maximum_fusion.1.refs_0_), channel_id=1, source_target_pairs={{0,3},{1,2},{2,1},{3,0},{4,7},{5,6},{6,5},{7,4},{8,11},{9,10},{10,... | collective-permute-start | bytes 98312 | tf_op jit(solution)/shard_map/ppermute | solution.py:240
  48.7 22.1 %collective-permute-start.20 = (bf16[4,32,128]{2,1,0:T(8,128)(2,1)S(1)}, bf16[4,32,128]{2,1,0:T(8,128)(2,1)S(1)}, u32[]{:S(2)}, u32[]{:S(2)}) collective-permute-start(bf16[4,32,128]{2,1,0:T(8,128)(2,1)S(1)} %pad_maximum_fusion.1.refs_0_), channel_id=1, source_target_pairs={{0,2},{1,3},{2,0},{3,1},{4,6},{5,7},{6,4},{7,5},{8,10},{9,11},{10,... | collective-permute-start | bytes 98312 | tf_op jit(solution)/shard_map/ppermute | solution.py:240
  49.0 22.8 %collective-permute-start.19 = (bf16[4,32,128]{2,1,0:T(8,128)(2,1)S(1)}, bf16[4,32,128]{2,1,0:T(8,128)(2,1)S(1)}, u32[]{:S(2)}, u32[]{:S(2)}) collective-permute-start(bf16[4,32,128]{2,1,0:T(8,128)(2,1)S(1)} %pad_maximum_fusion.1.refs_0_), channel_id=1, source_target_pairs={{0,1},{1,0},{2,3},{3,2},{4,5},{5,4},{6,7},{7,6},{8,9},{9,8},{10,11... | collective-permute-start | bytes 98312 | tf_op jit(solution)/shard_map/ppermute | solution.py:240
  49.6 22.2 %collective-permute-start.1 = (bf16[512,128]{1,0:T(8,128)(2,1)S(1)}, bf16[512,128]{1,0:T(8,128)(2,1)S(1)}, u32[]{:S(2)}, u32[]{:S(2)}) collective-permute-start(bf16[512,128]{1,0:T(8,128)(2,1)S(1)} %collective-permute-done.refs_0_), channel_id=1, source_target_pairs={{0,1},{1,0},{2,3},{3,2},{4,5},{5,4},{6,7},{7,6},{8,9},{9,8},{10,11... | collective-permute-start | bytes 393224 | tf_op jit(solution)/shard_map/ppermute | solution.py:240
  67.0 29.8 %collective-permute-start.43 = (bf16[96,128]{1,0:T(8,128)(2,1)S(1)}, bf16[96,128]{1,0:T(8,128)(2,1)S(1)}, u32[]{:S(2)}, u32[]{:S(2)}) collective-permute-start(bf16[96,128]{1,0:T(8,128)(2,1)S(1)} %get-tuple-element.15), channel_id=1, source_target_pairs={{0,25},{1,24},{2,17},{3,16},{4,9},{5,8},{6,1},{7,0},{8,27},{9,26},... | collective-permute-start | bytes 73736 | tf_op jit(solution)/shard_map/ppermute | solution.py:265
  67.1 33.4 %collective-permute-start.41 = (bf16[96,128]{1,0:T(8,128)(2,1)S(1)}, bf16[96,128]{1,0:T(8,128)(2,1)S(1)}, u32[]{:S(2)}, u32[]{:S(2)}) collective-permute-start(bf16[96,128]{1,0:T(8,128)(2,1)S(1)} %get-tuple-element.15), channel_id=1, source_target_pairs={{0,17},{1,16},{2,25},{3,24},{4,1},{5,0},{6,9},{7,8},{8,19},{9,18},... | collective-permute-start | bytes 73736 | tf_op jit(solution)/shard_map/ppermute | solution.py:265
  70.8 20.3 %collective-permute-start.28 = (bf16[192,128]{1,0:T(8,128)(2,1)S(1)}, bf16[192,128]{1,0:T(8,128)(2,1)S(1)}, u32[]{:S(2)}, u32[]{:S(2)}) collective-permute-start(bf16[192,128]{1,0:T(8,128)(2,1)S(1)} %bitcast.27), channel_id=1, source_target_pairs={{0,24},{8,16},{16,8},{24,0},{1,25},{9,17},{17,9},{25,1},{2,26},{10... | collective-permute-start | bytes 147464 | tf_op jit(solution)/shard_map/ppermute | solution.py:237
  71.8 20.3 %collective-permute-start.27 = (bf16[192,128]{1,0:T(8,128)(2,1)S(1)}, bf16[192,128]{1,0:T(8,128)(2,1)S(1)}, u32[]{:S(2)}, u32[]{:S(2)}) collective-permute-start(bf16[192,128]{1,0:T(8,128)(2,1)S(1)} %bitcast.28), channel_id=1, source_target_pairs={{0,16},{8,24},{16,0},{24,8},{1,17},{9,25},{17,1},{25,9},{2,18},{10... | collective-permute-start | bytes 147464 | tf_op jit(solution)/shard_map/ppermute | solution.py:237
  71.9 21.2 %collective-permute-start.26 = (bf16[192,128]{1,0:T(8,128)(2,1)S(1)}, bf16[192,128]{1,0:T(8,128)(2,1)S(1)}, u32[]{:S(2)}, u32[]{:S(2)}) collective-permute-start(bf16[192,128]{1,0:T(8,128)(2,1)S(1)} %bitcast.29), channel_id=1, source_target_pairs={{0,8},{8,0},{16,24},{24,16},{1,9},{9,1},{17,25},{25,17},{2,10},{10... | collective-permute-start | bytes 147464 | tf_op jit(solution)/shard_map/ppermute | solution.py:237
  91.2 9.4 %collective-permute-start.8 = (f32[32,128]{1,0:T(8,128)}, f32[32,128]{1,0:T(8,128)S(1)}, u32[]{:S(2)}, u32[]{:S(2)}) collective-permute-start(f32[32,128]{1,0:T(8,128)} %shard_map.97), channel_id=1, source_target_pairs={{0,24},{8,16},{16,8},{24,0},{1,25},{9,17},{17,9},{25,1},{2,26},{10... | collective-permute-start | bytes 49160 | tf_op jit(solution)/shard_map/ppermute | solution.py:237
  92.2 10.7 %collective-permute-start.7 = (f32[32,128]{1,0:T(8,128)}, f32[32,128]{1,0:T(8,128)S(1)}, u32[]{:S(2)}, u32[]{:S(2)}) collective-permute-start(f32[32,128]{1,0:T(8,128)} %shard_map.97), channel_id=1, source_target_pairs={{0,16},{8,24},{16,0},{24,8},{1,17},{9,25},{17,1},{25,9},{2,18},{10... | collective-permute-start | bytes 49160 | tf_op jit(solution)/shard_map/ppermute | solution.py:237
  93.1 11.8 %collective-permute-start.6 = (f32[32,128]{1,0:T(8,128)}, f32[32,128]{1,0:T(8,128)S(1)}, u32[]{:S(2)}, u32[]{:S(2)}) collective-permute-start(f32[32,128]{1,0:T(8,128)} %shard_map.97), channel_id=1, source_target_pairs={{0,8},{8,0},{16,24},{24,16},{1,9},{9,1},{17,25},{25,17},{2,10},{10... | collective-permute-start | bytes 49160 | tf_op jit(solution)/shard_map/ppermute | solution.py:237
  96.8 36.9 %copy-start.29 = (bf16[96,128]{1,0:T(8,128)(2,1)}, bf16[96,128]{1,0:T(8,128)(2,1)S(1)}, u32[]{:S(2)}) copy-start(bf16[96,128]{1,0:T(8,128)(2,1)S(1)} %collective-permute-done.43.refs_23_) | copy-start | bytes 73732
  96.9 8.8 %collective-permute-start.39 = (bf16[96,128]{1,0:T(8,128)(2,1)S(1)}, bf16[96,128]{1,0:T(8,128)(2,1)S(1)}, u32[]{:S(2)}, u32[]{:S(2)}) collective-permute-start(bf16[96,128]{1,0:T(8,128)(2,1)S(1)} %get-tuple-element.15), channel_id=1, source_target_pairs={{0,9},{1,8},{2,1},{3,0},{4,25},{5,24},{6,17},{7,16},{8,11},{9,10},... | collective-permute-start | bytes 73736 | tf_op jit(solution)/shard_map/ppermute | solution.py:265
  100.5 33.2 %copy-start.30 = (bf16[96,128]{1,0:T(8,128)(2,1)}, bf16[96,128]{1,0:T(8,128)(2,1)S(1)}, u32[]{:S(2)}) copy-start(bf16[96,128]{1,0:T(8,128)(2,1)S(1)} %collective-permute-done.41.refs_21_) | copy-start | bytes 73732
  100.5 6.4 %collective-permute-start.37 = (bf16[96,128]{1,0:T(8,128)(2,1)S(1)}, bf16[96,128]{1,0:T(8,128)(2,1)S(1)}, u32[]{:S(2)}, u32[]{:S(2)}) collective-permute-start(bf16[96,128]{1,0:T(8,128)(2,1)S(1)} %get-tuple-element.15), channel_id=1, source_target_pairs={{0,1},{1,0},{2,9},{3,8},{4,17},{5,16},{6,25},{7,24},{8,3},{9,2},{1... | collective-permute-start | bytes 73736 | tf_op jit(solution)/shard_map/ppermute | solution.py:265
  100.5 7.8 %collective-permute-start.42 = (bf16[96,128]{1,0:T(8,128)(2,1)S(1)}, bf16[96,128]{1,0:T(8,128)(2,1)S(1)}, u32[]{:S(2)}, u32[]{:S(2)}) collective-permute-start(bf16[96,128]{1,0:T(8,128)(2,1)S(1)} %get-tuple-element.16), channel_id=1, source_target_pairs={{0,24},{1,25},{2,16},{3,17},{4,8},{5,9},{6,0},{7,1},{8,26},{9,27},... | collective-permute-start | bytes 73736 | tf_op jit(solution)/shard_map/ppermute | solution.py:265
  102.9 6.8 %collective-permute-start.40 = (bf16[96,128]{1,0:T(8,128)(2,1)S(1)}, bf16[96,128]{1,0:T(8,128)(2,1)S(1)}, u32[]{:S(2)}, u32[]{:S(2)}) collective-permute-start(bf16[96,128]{1,0:T(8,128)(2,1)S(1)} %get-tuple-element.16), channel_id=1, source_target_pairs={{0,16},{1,17},{2,24},{3,25},{4,0},{5,1},{6,8},{7,9},{8,18},{9,19},... | collective-permute-start | bytes 73736 | tf_op jit(solution)/shard_map/ppermute | solution.py:265
  104.9 15.5 %collective-permute-start.32 = (f32[128,128]{1,0:T(8,128)}, f32[128,128]{1,0:T(8,128)S(1)}, u32[]{:S(2)}, u32[]{:S(2)}) collective-permute-start(f32[128,128]{1,0:T(8,128)} %get-tuple-element.9.refs_8_), channel_id=1, source_target_pairs={{0,4},{1,5},{2,6},{3,7},{4,0},{5,1},{6,2},{7,3},{8,12},{9,13},{10,... | collective-permute-start | bytes 196616 | tf_op jit(solution)/shard_map/ppermute | solution.py:240
  105.7 28.1 %copy-start.1 = (f32[4,32,128]{2,1,0:T(8,128)}, f32[4,32,128]{2,1,0:T(8,128)S(1)}, u32[]{:S(2)}) copy-start(f32[4,32,128]{2,1,0:T(8,128)S(1)} %pad_maximum_fusion.refs_0_) | copy-start | bytes 196612
  105.7 28.1 %copy-start.31 = (bf16[96,128]{1,0:T(8,128)(2,1)}, bf16[96,128]{1,0:T(8,128)(2,1)S(1)}, u32[]{:S(2)}) copy-start(bf16[96,128]{1,0:T(8,128)(2,1)S(1)} %collective-permute-done.39.refs_19_) | copy-start | bytes 73732
  105.7 18.4 %collective-permute-start.30 = (f32[128,128]{1,0:T(8,128)}, f32[128,128]{1,0:T(8,128)S(1)}, u32[]{:S(2)}, u32[]{:S(2)}) collective-permute-start(f32[128,128]{1,0:T(8,128)} %get-tuple-element.9.refs_8_), channel_id=1, source_target_pairs={{0,2},{1,3},{2,0},{3,1},{4,6},{5,7},{6,4},{7,5},{8,10},{9,11},{10,... | collective-permute-start | bytes 196616 | tf_op jit(solution)/shard_map/ppermute | solution.py:240
  106.9 17.2 %collective-permute-start.29 = (f32[128,128]{1,0:T(8,128)}, f32[128,128]{1,0:T(8,128)S(1)}, u32[]{:S(2)}, u32[]{:S(2)}) collective-permute-start(f32[128,128]{1,0:T(8,128)} %get-tuple-element.9.refs_8_), channel_id=1, source_target_pairs={{0,1},{1,0},{2,3},{3,2},{4,5},{5,4},{6,7},{7,6},{8,9},{9,8},{10,11... | collective-permute-start | bytes 196616 | tf_op jit(solution)/shard_map/ppermute | solution.py:240
  108.3 19.5 %collective-permute-start.12 = (f32[4,32,128]{2,1,0:T(8,128)S(1)}, f32[4,32,128]{2,1,0:T(8,128)S(1)}, u32[]{:S(2)}, u32[]{:S(2)}) collective-permute-start(f32[4,32,128]{2,1,0:T(8,128)S(1)} %pad_maximum_fusion.refs_0_), channel_id=1, source_target_pairs={{0,4},{1,5},{2,6},{3,7},{4,0},{5,1},{6,2},{7,3},{8,12},{9,13},{10,... | collective-permute-start | bytes 196616 | tf_op jit(solution)/shard_map/ppermute | solution.py:240
  109.7 5.4 %collective-permute-start.38 = (bf16[96,128]{1,0:T(8,128)(2,1)S(1)}, bf16[96,128]{1,0:T(8,128)(2,1)S(1)}, u32[]{:S(2)}, u32[]{:S(2)}) collective-permute-start(bf16[96,128]{1,0:T(8,128)(2,1)S(1)} %get-tuple-element.16), channel_id=1, source_target_pairs={{0,8},{1,9},{2,0},{3,1},{4,24},{5,25},{6,16},{7,17},{8,10},{9,11},... | collective-permute-start | bytes 73736 | tf_op jit(solution)/shard_map/ppermute | solution.py:265
  115.0 6.6 %collective-permute-start.36 = (bf16[96,128]{1,0:T(8,128)(2,1)S(1)}, bf16[96,128]{1,0:T(8,128)(2,1)S(1)}, u32[]{:S(2)}, u32[]{:S(2)}) collective-permute-start(bf16[96,128]{1,0:T(8,128)(2,1)S(1)} %get-tuple-element.16), channel_id=1, source_target_pairs={{0,0},{1,1},{2,8},{3,9},{4,16},{5,17},{6,24},{7,25},{8,2},{9,3},{1... | collective-permute-start | bytes 73736 | tf_op jit(solution)/shard_map/ppermute | solution.py:265
  120.3 7.6 %collective-permute-start.34 = (f32[128,128]{1,0:T(8,128)S(1)}, f32[128,128]{1,0:T(8,128)S(1)}, u32[]{:S(2)}, u32[]{:S(2)}) collective-permute-start(f32[128,128]{1,0:T(8,128)S(1)} %collective-permute-done.32.refs_12_), channel_id=1, source_target_pairs={{0,2},{1,3},{2,0},{3,1},{4,6},{5,7},{6,4},{7,5},{8,10},{9,11},{10,... | collective-permute-start | bytes 196616 | tf_op jit(solution)/shard_map/ppermute | solution.py:240
  121.6 7.0 %collective-permute-start.33 = (f32[128,128]{1,0:T(8,128)S(1)}, f32[128,128]{1,0:T(8,128)S(1)}, u32[]{:S(2)}, u32[]{:S(2)}) collective-permute-start(f32[128,128]{1,0:T(8,128)S(1)} %collective-permute-done.32.refs_12_), channel_id=1, source_target_pairs={{0,1},{1,0},{2,3},{3,2},{4,5},{5,4},{6,7},{7,6},{8,9},{9,8},{10,11... | collective-permute-start | bytes 196616 | tf_op jit(solution)/shard_map/ppermute | solution.py:240
  124.0 4.7 %collective-permute-start.31 = (f32[128,128]{1,0:T(8,128)S(1)}, f32[128,128]{1,0:T(8,128)S(1)}, u32[]{:S(2)}, u32[]{:S(2)}) collective-permute-start(f32[128,128]{1,0:T(8,128)S(1)} %collective-permute-done.30.refs_10_), channel_id=1, source_target_pairs={{0,1},{1,0},{2,3},{3,2},{4,5},{5,4},{6,7},{7,6},{8,9},{9,8},{10,11... | collective-permute-start | bytes 196616 | tf_op jit(solution)/shard_map/ppermute | solution.py:240
  124.1 5.8 %collective-permute-start.10 = (f32[4,32,128]{2,1,0:T(8,128)S(1)}, f32[4,32,128]{2,1,0:T(8,128)S(1)}, u32[]{:S(2)}, u32[]{:S(2)}) collective-permute-start(f32[4,32,128]{2,1,0:T(8,128)S(1)} %pad_maximum_fusion.refs_0_), channel_id=1, source_target_pairs={{0,2},{1,3},{2,0},{3,1},{4,6},{5,7},{6,4},{7,5},{8,10},{9,11},{10,... | collective-permute-start | bytes 196616 | tf_op jit(solution)/shard_map/ppermute | solution.py:240
  127.8 3.1 %collective-permute-start.14 = (f32[4,32,128]{2,1,0:T(8,128)S(1)}, f32[4,32,128]{2,1,0:T(8,128)S(1)}, u32[]{:S(2)}, u32[]{:S(2)}) collective-permute-start(f32[4,32,128]{2,1,0:T(8,128)S(1)} %collective-permute-done.12.refs_4_), channel_id=1, source_target_pairs={{0,2},{1,3},{2,0},{3,1},{4,6},{5,7},{6,4},{7,5},{8,10},{9,11},{10,... | collective-permute-start | bytes 196616 | tf_op jit(solution)/shard_map/ppermute | solution.py:240
  127.9 4.9 %collective-permute-start.35 = (f32[128,128]{1,0:T(8,128)S(1)}, f32[128,128]{1,0:T(8,128)S(1)}, u32[]{:S(2)}, u32[]{:S(2)}) collective-permute-start(f32[128,128]{1,0:T(8,128)S(1)} %collective-permute-done.34.refs_14_), channel_id=1, source_target_pairs={{0,1},{1,0},{2,3},{3,2},{4,5},{5,4},{6,7},{7,6},{8,9},{9,8},{10,11... | collective-permute-start | bytes 196616 | tf_op jit(solution)/shard_map/ppermute | solution.py:240
  128.6 4.2 %collective-permute-start.9 = (f32[4,32,128]{2,1,0:T(8,128)S(1)}, f32[4,32,128]{2,1,0:T(8,128)S(1)}, u32[]{:S(2)}, u32[]{:S(2)}) collective-permute-start(f32[4,32,128]{2,1,0:T(8,128)S(1)} %pad_maximum_fusion.refs_0_), channel_id=1, source_target_pairs={{0,1},{1,0},{2,3},{3,2},{4,5},{5,4},{6,7},{7,6},{8,9},{9,8},{10,11... | collective-permute-start | bytes 196616 | tf_op jit(solution)/shard_map/ppermute | solution.py:240
  128.7 4.1 %collective-permute-start.13 = (f32[4,32,128]{2,1,0:T(8,128)S(1)}, f32[4,32,128]{2,1,0:T(8,128)S(1)}, u32[]{:S(2)}, u32[]{:S(2)}) collective-permute-start(f32[4,32,128]{2,1,0:T(8,128)S(1)} %collective-permute-done.12.refs_4_), channel_id=1, source_target_pairs={{0,1},{1,0},{2,3},{3,2},{4,5},{5,4},{6,7},{7,6},{8,9},{9,8},{10,11... | collective-permute-start | bytes 196616 | tf_op jit(solution)/shard_map/ppermute | solution.py:240
  129.9 2.9 %collective-permute-start.11 = (f32[4,32,128]{2,1,0:T(8,128)S(1)}, f32[4,32,128]{2,1,0:T(8,128)S(1)}, u32[]{:S(2)}, u32[]{:S(2)}) collective-permute-start(f32[4,32,128]{2,1,0:T(8,128)S(1)} %collective-permute-done.10.refs_2_), channel_id=1, source_target_pairs={{0,1},{1,0},{2,3},{3,2},{4,5},{5,4},{6,7},{7,6},{8,9},{9,8},{10,11... | collective-permute-start | bytes 196616 | tf_op jit(solution)/shard_map/ppermute | solution.py:240
  131.0 2.8 %collective-permute-start.15 = (f32[4,32,128]{2,1,0:T(8,128)S(1)}, f32[4,32,128]{2,1,0:T(8,128)S(1)}, u32[]{:S(2)}, u32[]{:S(2)}) collective-permute-start(f32[4,32,128]{2,1,0:T(8,128)S(1)} %collective-permute-done.14.refs_6_), channel_id=1, source_target_pairs={{0,1},{1,0},{2,3},{3,2},{4,5},{5,4},{6,7},{7,6},{8,9},{9,8},{10,11... | collective-permute-start | bytes 196616 | tf_op jit(solution)/shard_map/ppermute | solution.py:240
  (39 other events, 439.7 us)

commit v2 on v1

v2 whole, which is shorter than its diff:
```python
import functools

import jax
import jax.numpy as jnp
from jax import lax
from jax.experimental import pallas as pl
from jax.experimental.pallas import tpu as pltpu
from jax.sharding import PartitionSpec as P

NEG = -1e30
SCALE = 4.0
TILE = 16
GROUP = 32
LANES = 128


def params(megabytes):
    return pltpu.CompilerParams(vmem_limit_bytes=megabytes * 1024 * 1024)


def vmem():
    return pl.BlockSpec(memory_space=pltpu.VMEM)


def smem():
    return pl.BlockSpec(memory_space=pltpu.SMEM)


def split(x, parts):
    out = []
    for _ in range(parts):
        piece = x.astype(jnp.bfloat16)
        out.append(piece)
        x = x - piece.astype(jnp.float32)
    return out


def mxu(a, b, dims=((1,), (0,))):
    return lax.dot_general(a, b, (dims, ((), ())), preferred_element_type=jnp.float32)


def live_blocks(lengths_ref, blocks_ref, passages, per):
    def one(p, at):
        for b in range(per):
            blocks_ref[at + b] = p * TILE + b
        return at + (lengths_ref[p] + TILE - 1) // TILE

    count = lax.fori_loop(0, passages, one, 0)
    for i in range(GROUP):
        blocks_ref[count + i] = (passages - 1) * TILE
    return count


def teacher_kernel(slots, shift, sides, first, *refs):
    query_ref = refs[0]
    token_refs = refs[1 : 1 + len(sides)]
    length_refs = refs[1 + len(sides) : 1 + 2 * len(sides)]
    prior_ref = None if first else refs[1 + 2 * len(sides)]
    out_ref, flipped, best, blocks_ref = refs[-4:]
    passages, lanes = out_ref.shape
    rows = query_ref.shape[0]
    tile = min(256, rows)
    r, c = lax.axis_index("row"), lax.axis_index("col")
    flipped[...] = query_ref[...].astype(jnp.float32).T.astype(jnp.bfloat16)
    total = jnp.zeros(out_ref.shape, jnp.float32) if first else prior_ref[...]
    sub = lax.broadcasted_iota(jnp.int32, (8, tile), 0)
    for side, tokens_ref, lengths_ref in zip(sides, token_refs, length_refs):
        per = tokens_ref.shape[0] // passages
        count = live_blocks(lengths_ref, blocks_ref, passages, per)
        best[...] = jnp.full(best.shape, NEG, jnp.float32)

        def step(i, carry, tokens_ref=tokens_ref, lengths_ref=lengths_ref, per=per):
            owner, begin, values = [], [], []
            for g in range(GROUP):
                entry = blocks_ref[i * GROUP + g]
                p, b = entry // TILE, entry % TILE
                owner.append(pl.multiple_of(p * 8, 8))
                begin.append(lengths_ref[p] - b * TILE)
                values.append(tokens_ref[p * per + b])
            block = jnp.concatenate(values, axis=0)
            for n in range(0, rows, tile):
                sims = mxu(block, flipped[:, n : n + tile])
                for g in range(GROUP):
                    top = jnp.where(sub < begin[g], sims[g * TILE : g * TILE + 8], NEG)
                    low = jnp.where(sub < begin[g] - 8, sims[g * TILE + 8 : g * TILE + 16], NEG)
                    peak = jnp.maximum(top, low)
                    for l in range(0, tile, LANES):
                        at = ((n + l) // LANES, pl.ds(owner[g], 8))
                        best[at] = jnp.maximum(best[at], peak[:, l : l + LANES])
            return carry

        lax.fori_loop(0, (count + GROUP - 1) // GROUP, step, 0)
        found = []
        for l in range(rows // LANES):
            peak = best[l, pl.ds(0, passages, stride=8), :]
            for s in range(1, 8):
                peak = jnp.maximum(peak, best[l, pl.ds(s, passages, stride=8), :])
            found.append(peak)
        found = jnp.concatenate(found, axis=1)
        parity = c % 2 if side == 0 else 1 - c % 2
        start = parity * (lanes // 2) + (r ^ shift) * (rows // slots)
        owner = lax.broadcasted_iota(jnp.int32, (rows, lanes), 0) // slots + start
        member = (owner == lax.broadcasted_iota(jnp.int32, (rows, lanes), 1)).astype(jnp.bfloat16)
        for piece in split(found, 3):
            total = total + mxu(piece, member)
    out_ref[...] = total


def teacher_block(query, slots, shift, sides, tokens, lengths, prior, queries, passages):
    tokens = [tokens[side] for side in sides]
    operands = [query] + tokens + [lengths[side] for side in sides]
    specs = [vmem()] * (1 + len(sides)) + [smem()] * len(sides)
    if prior is not None:
        operands.append(prior)
        specs.append(vmem())
    rows, width = query.shape
    return pl.pallas_call(
        functools.partial(teacher_kernel, slots, shift, sides, prior is None),
        out_shape=jax.ShapeDtypeStruct((passages, queries), jnp.float32),
        in_specs=specs,
        out_specs=vmem(),
        scratch_shapes=[
            pltpu.VMEM((width, rows), jnp.bfloat16),
            pltpu.VMEM((rows // LANES, passages * 8, LANES), jnp.float32),
            pltpu.SMEM((tokens[0].shape[0] + TILE + GROUP,), jnp.int32),
        ],
        compiler_params=params(16),
        cost_estimate=pl.CostEstimate(
            flops=2 * rows * sum(t.size for t in tokens),
            bytes_accessed=2 * sum(t.size for t in tokens),
            transcendentals=0,
        ),
    )(*operands)


def student_kernel(R, C, wide, sq_ref, *refs):
    sp_refs, cut_refs = refs[:R], refs[R:-4]
    sent_ref, vectors_ref, pos_ref, held = refs[-4:]
    per = C // R
    r, c = lax.axis_index("row"), lax.axis_index("col")
    lanes = sq_ref.shape[2]
    half = sq_ref.shape[1] // 2
    queries = 2 * R * half
    span = sp_refs[0].shape[1]

    def columns(index):
        for i in range(R):
            for h in range(2):
                held[h, i] = sq_ref[i * C + index, h * half : (h + 1) * half]
        return held[...].reshape(queries, lanes).astype(jnp.float32)

    total = jnp.zeros((queries, span), jnp.float32)
    for k in range(R):
        pieces = [columns((r ^ k) * per + h)[:, :wide] for h in range(per)]
        vectors = jnp.concatenate(pieces, axis=1).astype(jnp.bfloat16)
        if k == 0:
            vectors_ref[...] = vectors
        total = total + mxu(vectors, sp_refs[k][...])
    scores = split((SCALE * total).T, 3)
    pad = sent_ref.shape[1] - 3 * span * (queries // LANES)
    for i in range(C):
        at = pad
        for piece in scores:
            for n in range(0, queries, LANES):
                sent_ref[i, at : at + span] = piece[:, n : n + LANES]
                at += span
    for k in range(R):
        for h in range(per):
            cut = cut_refs[0][k, h] if cut_refs else sp_refs[k][h * wide : (h + 1) * wide]
            sent_ref[(r ^ k) * per + h, :pad] = cut
    meta = columns(c)
    where = meta[:, wide : wide + 1] * 64.0 + meta[:, wide + 1 : wide + 2]
    diag = lax.broadcasted_iota(jnp.int32, (queries, queries), 0) == lax.broadcasted_iota(
        jnp.int32, (queries, queries), 1
    )
    pos_ref[...] = jnp.sum(jnp.where(diag, where, 0.0), axis=0, keepdims=True)


def student_scores(sq, sp, R, C, wide):
    block, lanes = sq.shape[1:]
    queries, depth, span = R * block, sp[0].shape[0], sp[0].shape[1]
    per = C // R
    pad = wide + -wide % TILE
    cut = []
    if pad > wide:
        cut = [jnp.pad(jnp.stack(sp).reshape(R, per, wide, span), ((0, 0), (0, 0), (0, pad - wide), (0, 0)))]
    return pl.pallas_call(
        functools.partial(student_kernel, R, C, wide),
        out_shape=(
            jax.ShapeDtypeStruct((C, pad + 3 * span * (queries // LANES), LANES), jnp.bfloat16),
            jax.ShapeDtypeStruct((queries, depth), jnp.bfloat16),
            jax.ShapeDtypeStruct((1, queries), jnp.float32),
        ),
        in_specs=[vmem()] * (1 + R + len(cut)),
        out_specs=(vmem(),) * 3,
        scratch_shapes=[pltpu.VMEM((2, R, block // 2, lanes), jnp.bfloat16)],
        compiler_params=params(40),
    )(sq, *sp, *cut)


def finish_kernel(R, C, block, wide, t_ref, s_ref, vectors_ref, pos_ref, query_ref, passage_ref, loss_ref, teach, stud):
    r, c = lax.axis_index("row"), lax.axis_index("col")
    queries = pos_ref.shape[1]
    span = passage_ref.shape[1]
    pad = s_ref.shape[1] - 3 * span * (queries // LANES)
    half = queries // 2
    shape = (span, queries)

    def rows(op, x):
        return op(x, axis=0, keepdims=True)

    def peak(j, carry):
        t_max, s_max = carry
        pair = [t_ref[2 * j + h].reshape(span, queries) for h in range(2)]
        for b in range(2):
            t = jnp.concatenate([x[:, b * half : (b + 1) * half] for x in pair], axis=1)
            teach[2 * j + b] = t
            t_max = jnp.maximum(t_max, t)
            pieces, at = [], pad
            for _ in range(3):
                cells = []
                for _ in range(0, queries, LANES):
                    cells.append(s_ref[2 * j + b, at : at + span].astype(jnp.float32))
                    at += span
                pieces.append(jnp.concatenate(cells, axis=1))
            s = pieces[0] + (pieces[1] + pieces[2])
            stud[2 * j + b] = s
            s_max = jnp.maximum(s_max, s)
        return t_max, s_max

    low = jnp.full(shape, -jnp.inf, jnp.float32)
    t_max, s_max = lax.fori_loop(0, C // 2, peak, (low, low))
    t_max, s_max = rows(jnp.max, t_max), rows(jnp.max, s_max)
    place = pos_ref[...].astype(jnp.int32)
    index = lax.broadcasted_iota(jnp.int32, shape, 0)

    def totals(i, carry):
        t_sum, s_sum, cross, score = carry
        t, s = teach[i], stud[i]
        t_exp, s_exp = jnp.exp(t - t_max), jnp.exp(s - s_max)
        hot = index + i * span == place
        teach[i] = t_exp
        stud[i] = s_exp
        return (
            t_sum + rows(jnp.sum, t_exp),
            s_sum + rows(jnp.sum, s_exp),
            cross + rows(jnp.sum, t_exp * (t - s)),
            score + rows(jnp.sum, jnp.where(hot, s, 0.0)),
        )

    zero = jnp.zeros((1, queries), jnp.float32)
    t_sum, s_sum, cross, score = lax.fori_loop(0, C, totals, (zero,) * 4)
    t_lse = t_max + jnp.log(t_sum)
    s_lse = s_max + jnp.log(s_sum)
    each = cross / t_sum - t_lse + 2.0 * s_lse - score
    loss_ref[...] = jnp.sum(each, axis=1, keepdims=True) / queries
    factor = SCALE / queries
    t_factor, s_factor = factor / t_sum, 2.0 * factor / s_sum

    def slope(i):
        hot = index + i * span == place
        gap = stud[i] * s_factor - teach[i] * t_factor
        return split(gap - jnp.where(hot, factor, 0.0), 2)

    def gradient(i, total):
        for piece in slope(i):
            total = total + mxu(s_ref[i, :pad], piece)
        return total

    flat = lax.fori_loop(0, C, gradient, jnp.zeros((pad, queries), jnp.float32)).T[:, :wide]
    sub = block // 2
    for h in range(2):
        query_ref[h * sub : (h + 1) * sub, :] = functools.reduce(
            jnp.add,
            [jnp.where(r == i, flat[h * half + i * sub : h * half + (i + 1) * sub], 0.0) for i in range(R)],
        )
    grads = sum(mxu(piece, vectors_ref[...]) for piece in slope(c))
    passage_ref[...] = grads.T


def finish(t, s, vectors, pos, R, C, block, wide, span):
    queries = pos.shape[1]
    held = pltpu.VMEM((C, span, queries), jnp.float32)
    return pl.pallas_call(
        functools.partial(finish_kernel, R, C, block, wide),
        out_shape=(
            jax.ShapeDtypeStruct((block, wide), jnp.float32),
            jax.ShapeDtypeStruct((vectors.shape[1], span), jnp.float32),
            jax.ShapeDtypeStruct((1, 1), jnp.float32),
        ),
        in_specs=[vmem()] * 4,
        out_specs=(vmem(),) * 3,
        scratch_shapes=[held, held],
        compiler_params=params(48),
    )(t, s, vectors, pos)


def shards(query_tokens, query_lengths, passage_tokens, passage_lengths, student_queries, student_passages, positives):
    R, C = lax.axis_size("row"), lax.axis_size("col")
    r, c = lax.axis_index("row"), lax.axis_index("col")
    block, slots, width = query_tokens.shape
    queries = block * R
    local, count = passage_tokens.shape[:2]
    half = block // 2

    def over_row(x, k):
        return lax.ppermute(x, "row", [(i, i ^ k) for i in range(R)])

    def over_col(x, k):
        return lax.ppermute(x, "col", [(i, i ^ k) for i in range(C)])

    part = lax.dynamic_slice_in_dim(query_tokens, (c % 2) * half, half, 0)
    lives = lax.dynamic_slice_in_dim(query_lengths, (c % 2) * half, half, 0)
    live = jnp.arange(slots)[None, :] < lives[:, None]
    mine = jnp.where(live[:, :, None], part, 0).reshape(half * slots, width)
    near = [mine] + [over_row(mine, k) for k in range(1, R)]
    cells = passage_tokens.reshape(local * count // TILE, TILE, width)
    tokens = [cells, over_col(cells, 1)]
    lengths = [passage_lengths, over_col(passage_lengths, 1)]

    wide = student_queries.shape[1]
    meta = jnp.stack([positives // 64, positives % 64], axis=1).astype(jnp.bfloat16)
    sent = jnp.pad(jnp.concatenate([student_queries, meta], axis=1), ((0, 0), (0, -(wide + 2) % LANES)))
    sq = lax.all_to_all(jnp.broadcast_to(sent[None], (R * C,) + sent.shape), ("row", "col"), 0, 0, tiled=True)
    flipped = student_passages.T
    sp = [flipped] + [over_row(flipped, k) for k in range(1, R)]

    common = dict(slots=slots, tokens=tokens, lengths=lengths, queries=queries, passages=local)
    score = teacher_block(near[0], shift=0, sides=(0,), prior=None, **common)
    score = teacher_block(near[0], shift=0, sides=(1,), prior=score, **common)
    out, vectors, pos = student_scores(sq, sp, R, C, wide)
    s = lax.all_to_all(out, "col", 0, 0, tiled=True)
    for k in range(1, R):
        score = teacher_block(near[k], shift=k, sides=(0, 1), prior=score, **common)
    t = lax.all_gather(score, ("col", "row"), axis=0, tiled=True).reshape(C, R * local, queries)
    span = R * local
    query_grads, passage_grads, loss = finish(t, s, vectors, pos, R, C, block, wide, span)
    return (query_grads, passage_grads.T, loss[0, 0])


def solution(mesh):
    return jax.shard_map(
        shards,
        mesh=mesh,
        in_specs=(
            P("row", None, None),
            P("row"),
            P(("col", "row"), None, None),
            P(("col", "row")),
            P("row", "col"),
            P("col", "row"),
            P("row"),
        ),
        out_specs=(P("row", "col"), P("col", "row"), P()),
        check_vma=False,
    )
```

time: 138 us -> 160 us (1.16)
  the two profiles are of different devices: /device:TPU:5 before, /device:TPU:0 now
where the time goes in v2:
time: 160 us; the launch traced here: 161 us
  blocking collectives  72.7 us (45%)
  Pallas kernels  55.2 us (34%)
  starting transfers between devices  20.1 us (13%)
  waiting for transfers between devices  7.77 us (5%)
  local copies, waits for them, and re-layouts  2.49 us (2%)
  other arithmetic  1.66 us (1%)
    all_gather x1, blocking collectives, shards(): lax.all_gather(score, ('col', 'row'), axis=0, tiled=True)  72.7 us
    pallas_call x5, Pallas kernels, teacher_block(): pl.pallas_call(functools.partial(teacher_kernel, slots, shift, sides, pri...  50.8 us
    ppermute x6, starting transfers between devices, over_row(): return lax.ppermute(x, 'row', [(i, i ^ k) for i in range(R)])  8.9 us
    ppermute x6, waiting for transfers between devices, over_row(): return lax.ppermute(x, 'row', [(i, i ^ k) for i in range(R)])  7.76 us
    all_to_all x1, starting transfers between devices, shards(): lax.all_to_all(jnp.broadcast_to(sent[None], (R * C,) + sent.shape), ('row...  6.96 us
    all_to_all x1, starting transfers between devices, shards(): s = lax.all_to_all(out, 'col', 0, 0, tiled=True)  3.67 us
  transfers between devices with their start and end apart: 10, of which 2 were waited for; matrix products, arithmetic and copies ran while one was open for 2% of the time, Pallas kernels for 32%

profile of v2, /device:TPU:0, one launch (start us, length us, event | category | flops | bytes accessed | tf_op | source)
XLA Modules:
  0.0 160.6 jit_solution(8210610067281268459)
XLA Ops:
  0.6 0.5 collective-permute-start.1
  1.1 0.7 convert_bitcast_fusion
  1.8 0.1 copy.10
  1.9 0.1 copy.11
  2.0 0.8 fusion.4
  2.8 0.7 broadcast_in_dim.23
  3.5 0.0 copy-start.3
  3.5 7.0 %all-to-all-start = ((bf16[32,32,128]{2,1,0:T(8,128)(2,1)}), bf16[32,32,128]{2,1,0:T(8,128)(2,1)S(1)}, u32[]{:S(2)}, u32[]{:S(2)}) async-start(bf16[32,32,128]{2,1,0:T(8,128)(2,1)} %broadcast_in_dim.23), calls=%async_computation | async-start | bytes 524288 | tf_op jit(solution)/shard_map/all_to_all | solution.py:324
  10.5 0.0 copy-start.2
  10.5 1.8 %collective-permute-start.5 = (bf16[192,128]{1,0:T(8,128)(2,1)}, bf16[192,128]{1,0:T(8,128)(2,1)S(1)}, u32[]{:S(2)}, u32[]{:S(2)}) collective-permute-start(bf16[192,128]{1,0:T(8,128)(2,1)} %bitcast.16), channel_id=1, source_target_pairs={{0,8},{8,0},{16,24},{24,16},{1,9},{9,1},{17,25},{25,17},{2,10},{10... | collective-permute-start | bytes 147464 | tf_op jit(solution)/shard_map/ppermute | solution.py:307
  12.4 2.4 %collective-permute-start.6 = (bf16[192,128]{1,0:T(8,128)(2,1)}, bf16[192,128]{1,0:T(8,128)(2,1)S(1)}, u32[]{:S(2)}, u32[]{:S(2)}) collective-permute-start(bf16[192,128]{1,0:T(8,128)(2,1)} %bitcast.17), channel_id=1, source_target_pairs={{0,16},{8,24},{16,0},{24,8},{1,17},{9,25},{17,1},{25,9},{2,18},{10... | collective-permute-start | bytes 147464 | tf_op jit(solution)/shard_map/ppermute | solution.py:307
  14.8 0.2 collective-permute-start.7
  15.0 0.7 dynamic_slice.6
  15.7 0.1 iota_compare_fusion.1
  15.8 1.5 collective-permute-done.5.refs_1_
  17.2 6.3 %collective-permute-done.6.refs_2_ = bf16[192,128]{1,0:T(8,128)(2,1)S(1)} collective-permute-done((bf16[192,128]{1,0:T(8,128)(2,1)}, bf16[192,128]{1,0:T(8,128)(2,1)S(1)}, u32[]{:S(2)}, u32[]{:S(2)}) %collective-permute-start.6) | collective-permute-done | bytes 49184 | tf_op jit(solution)/shard_map/ppermute | solution.py:307
  23.5 0.0 collective-permute-done.7.refs_3_
  23.5 0.0 all-to-all-done.sq_ref
  23.5 0.0 copy-start
  23.5 0.8 copy-done
  24.3 0.0 copy-start.1
  24.3 1.4 shard_map.99
  25.7 3.7 %all-to-all-start.1 = ((bf16[8,480,128]{2,1,0:T(8,128)(2,1)}), bf16[8,480,128]{2,1,0:T(8,128)(2,1)S(1)}, u32[]{:S(2)}, u32[]{:S(2)}) async-start(bf16[8,480,128]{2,1,0:T(8,128)(2,1)} %get-tuple-element.9), calls=%async_computation.1 | async-start | bytes 1966080 | tf_op jit(solution)/shard_map/all_to_all | solution.py:332
  29.4 0.0 copy-done.3
  29.4 0.1 dynamic-slice_select_fusion
  29.5 1.2 collective-permute-start.4
  30.7 0.5 collective-permute-start.3
  31.3 2.7 %collective-permute-start = (bf16[512,128]{1,0:T(8,128)(2,1)S(1)}, bf16[512,128]{1,0:T(8,128)(2,1)S(1)}, u32[]{:S(2)}, u32[]{:S(2)}) collective-permute-start(bf16[512,128]{1,0:T(8,128)(2,1)S(1)} %bitcast.13), channel_id=1, source_target_pairs={{0,24},{8,16},{16,8},{24,0},{1,25},{9,17},{17,9},{25,1},{2,26},{10... | collective-permute-start | bytes 393224 | tf_op jit(solution)/shard_map/ppermute | solution.py:307
  34.0 0.0 copy-done.2
  34.0 0.0 collective-permute-start.2
  34.0 0.0 copy-done.1
  34.0 5.9 %shard_map.94.refs_3_ = f32[32,128]{1,0:T(8,128)S(1)} custom-call(bf16[512,128]{1,0:T(8,128)(2,1)S(1)} %bitcast.14, bf16[352,16,128]{2,1,0:T(8,128)(2,1)S(1)} %bitcast.21, s32[32]{0:T(128)S(1)} %copy-done.2), custom_call_target="tpu_custom_call" | custom-call | flops 738197504 | bytes 1441792 | tf_op jit(solution)/shard_map/pallas_call | solution.py:117
  39.9 0.0 collective-permute-done.2.refs_2_.refs_4_
  39.9 0.0 collective-permute-done.1.refs_1_.refs_2_
  39.9 7.3 %shard_map.95.refs_5_ = f32[32,128]{1,0:T(8,128)S(1)} custom-call(bf16[512,128]{1,0:T(8,128)(2,1)S(1)} %bitcast.15, bf16[352,16,128]{2,1,0:T(8,128)(2,1)} %collective-permute-done.1.refs_1_.refs_2_, s32[32]{0:T(128)S(1)} %collective-permute-done.2.refs_2_.refs_4_, f32[32,128]{1,0:T(8,128)S(1)} %shard_map.94.refs_3_), custom_call_target="tpu_custom_call" | custom-call | flops 738197504 | bytes 1441792 | tf_op jit(solution)/shard_map/pallas_call | solution.py:117
  47.2 0.0 collective-permute-done.4.refs_0_
  47.2 12.5 %shard_map.96.refs_5_ = f32[32,128]{1,0:T(8,128)S(1)} custom-call(bf16[512,128]{1,0:T(8,128)(2,1)S(1)} %collective-permute-done.4.refs_0_, bf16[352,16,128]{2,1,0:T(8,128)(2,1)S(1)} %bitcast.22, bf16[352,16,128]{2,1,0:T(8,128)(2,1)} %collective-permute-done.1.refs_1_.refs_2_, s32[32]{0:T(128)S(1)} %copy-done.2, ...), custom_call_target="tpu_custom_call" | custom-call | flops 1476395008 | bytes 2883584 | tf_op jit(solution)/shard_map/pallas_call | solution.py:117
  59.8 0.0 collective-permute-done.3.refs_0_
  59.8 12.5 %shard_map.97.refs_5_ = f32[32,128]{1,0:T(8,128)S(1)} custom-call(bf16[512,128]{1,0:T(8,128)(2,1)S(1)} %collective-permute-done.3.refs_0_, bf16[352,16,128]{2,1,0:T(8,128)(2,1)S(1)} %bitcast.23, bf16[352,16,128]{2,1,0:T(8,128)(2,1)} %collective-permute-done.1.refs_1_.refs_2_, s32[32]{0:T(128)S(1)} %copy-done.2, ...), custom_call_target="tpu_custom_call" | custom-call | flops 1476395008 | bytes 2883584 | tf_op jit(solution)/shard_map/pallas_call | solution.py:117
  72.3 0.0 collective-permute-done.refs_0_
  72.3 12.5 %shard_map.98 = f32[32,128]{1,0:T(8,128)S(1)} custom-call(bf16[512,128]{1,0:T(8,128)(2,1)S(1)} %collective-permute-done.refs_0_, bf16[352,16,128]{2,1,0:T(8,128)(2,1)S(1)} %bitcast.24, bf16[352,16,128]{2,1,0:T(8,128)(2,1)} %collective-permute-done.1.refs_1_.refs_2_, s32[32]{0:T(128)S(1)} %copy-done.2, s32[32]{0:T(128)S(1)} %collective-permute-done.2.refs_2_.refs_4_, ...), custom_call_target="tpu_custom_call" | custom-call | flops 1476395008 | bytes 2883584 | tf_op jit(solution)/shard_map/pallas_call | solution.py:117
  84.8 72.7 %all_gather.3 = f32[1024,128]{1,0:T(8,128)S(1)} all-gather(f32[32,128]{1,0:T(8,128)S(1)} %shard_map.98), channel_id=1, replica_groups=mesh['row'=4,'col'=8] {'col','row'}, dimensions={0}, use_global_device_ids=true | all-gather | bytes 540672 | tf_op jit(solution)/shard_map/all_gather | solution.py:335
  157.6 0.0 all-to-all-done.1.s_ref
  157.6 3.0 %shard_map.100 = (f32[32,96]{1,0:T(8,128)}, f32[192,128]{1,0:T(8,128)}, f32[1,1]{1,0:T(1,128)}) custom-call(f32[8,128,128]{2,1,0:T(8,128)S(1)} %bitcast.10, bf16[8,480,128]{2,1,0:T(8,128)(2,1)S(1)} %all-to-all-done.1.s_ref, bf16[128,192]{1,0:T(8,128)(2,1)S(1)} %get-tuple-element.10.vectors_ref, f32[1,128]{1,0:T(1,128)S(1)} %get-tuple-element.11.pos_ref), custom_call_target="tpu_custom_call" | custom-call | tf_op jit(solution)/shard_map/pallas_call | solution.py:284
Async XLA Ops:
  0.6 39.3 %collective-permute-start.1 = (bf16[352,16,128]{2,1,0:T(8,128)(2,1)}, bf16[352,16,128]{2,1,0:T(8,128)(2,1)}, u32[]{:S(2)}, u32[]{:S(2)}) collective-permute-start(bf16[352,16,128]{2,1,0:T(8,128)(2,1)} %bitcast.20), channel_id=1, source_target_pairs={{0,1},{1,0},{2,3},{3,2},{4,5},{5,4},{6,7},{7,6},{8,9},{9,8},{10,11... | collective-permute-start | bytes 4325384 | tf_op jit(solution)/shard_map/ppermute | solution.py:310
  3.5 25.8 %copy-start.3 = (bf16[32,32,128]{2,1,0:T(8,128)(2,1)S(1)}, bf16[32,32,128]{2,1,0:T(8,128)(2,1)}, u32[]{:S(2)}) copy-start(bf16[32,32,128]{2,1,0:T(8,128)(2,1)} %param.7) | copy-start | bytes 786436
  3.5 20.0 %all-to-all-start = ((bf16[32,32,128]{2,1,0:T(8,128)(2,1)}), bf16[32,32,128]{2,1,0:T(8,128)(2,1)S(1)}, u32[]{:S(2)}, u32[]{:S(2)}) async-start(bf16[32,32,128]{2,1,0:T(8,128)(2,1)} %broadcast_in_dim.23), calls=%async_computation | async-start | bytes 524288 | tf_op jit(solution)/shard_map/all_to_all | solution.py:324
  10.5 23.5 %copy-start.2 = (s32[32]{0:T(128)S(1)}, s32[32]{0:T(128)}, u32[]{:S(2)}) copy-start(s32[32]{0:T(128)} %refs_3_.5) | copy-start | bytes 388
  10.5 6.7 %collective-permute-start.5 = (bf16[192,128]{1,0:T(8,128)(2,1)}, bf16[192,128]{1,0:T(8,128)(2,1)S(1)}, u32[]{:S(2)}, u32[]{:S(2)}) collective-permute-start(bf16[192,128]{1,0:T(8,128)(2,1)} %bitcast.16), channel_id=1, source_target_pairs={{0,8},{8,0},{16,24},{24,16},{1,9},{9,1},{17,25},{25,17},{2,10},{10... | collective-permute-start | bytes 147464 | tf_op jit(solution)/shard_map/ppermute | solution.py:307
  12.4 11.2 %collective-permute-start.6 = (bf16[192,128]{1,0:T(8,128)(2,1)}, bf16[192,128]{1,0:T(8,128)(2,1)S(1)}, u32[]{:S(2)}, u32[]{:S(2)}) collective-permute-start(bf16[192,128]{1,0:T(8,128)(2,1)} %bitcast.17), channel_id=1, source_target_pairs={{0,16},{8,24},{16,0},{24,8},{1,17},{9,25},{17,1},{25,9},{2,18},{10... | collective-permute-start | bytes 147464 | tf_op jit(solution)/shard_map/ppermute | solution.py:307
  14.8 8.8 %collective-permute-start.7 = (bf16[192,128]{1,0:T(8,128)(2,1)}, bf16[192,128]{1,0:T(8,128)(2,1)S(1)}, u32[]{:S(2)}, u32[]{:S(2)}) collective-permute-start(bf16[192,128]{1,0:T(8,128)(2,1)} %bitcast.18), channel_id=1, source_target_pairs={{0,24},{8,16},{16,8},{24,0},{1,25},{9,17},{17,9},{25,1},{2,26},{10... | collective-permute-start | bytes 147464 | tf_op jit(solution)/shard_map/ppermute | solution.py:307
  23.5 0.8 copy-start
  24.3 9.7 %copy-start.1 = (bf16[32,176,128]{2,1,0:T(8,128)(2,1)S(1)}, bf16[32,176,128]{2,1,0:T(8,128)(2,1)}, u32[]{:S(2)}) copy-start(bf16[32,176,128]{2,1,0:T(8,128)(2,1)} %param.9) | copy-start | bytes 4325380
  25.7 131.9 %all-to-all-start.1 = ((bf16[8,480,128]{2,1,0:T(8,128)(2,1)}), bf16[8,480,128]{2,1,0:T(8,128)(2,1)S(1)}, u32[]{:S(2)}, u32[]{:S(2)}) async-start(bf16[8,480,128]{2,1,0:T(8,128)(2,1)} %get-tuple-element.9), calls=%async_computation.1 | async-start | bytes 1966080 | tf_op jit(solution)/shard_map/all_to_all | solution.py:332
  29.5 17.7 %collective-permute-start.4 = (bf16[512,128]{1,0:T(8,128)(2,1)S(1)}, bf16[512,128]{1,0:T(8,128)(2,1)S(1)}, u32[]{:S(2)}, u32[]{:S(2)}) collective-permute-start(bf16[512,128]{1,0:T(8,128)(2,1)S(1)} %bitcast.11), channel_id=1, source_target_pairs={{0,8},{8,0},{16,24},{24,16},{1,9},{9,1},{17,25},{25,17},{2,10},{10... | collective-permute-start | bytes 393224 | tf_op jit(solution)/shard_map/ppermute | solution.py:307
  30.7 29.0 %collective-permute-start.3 = (bf16[512,128]{1,0:T(8,128)(2,1)S(1)}, bf16[512,128]{1,0:T(8,128)(2,1)S(1)}, u32[]{:S(2)}, u32[]{:S(2)}) collective-permute-start(bf16[512,128]{1,0:T(8,128)(2,1)S(1)} %bitcast.12), channel_id=1, source_target_pairs={{0,16},{8,24},{16,0},{24,8},{1,17},{9,25},{17,1},{25,9},{2,18},{10... | collective-permute-start | bytes 393224 | tf_op jit(solution)/shard_map/ppermute | solution.py:307
  31.3 41.0 %collective-permute-start = (bf16[512,128]{1,0:T(8,128)(2,1)S(1)}, bf16[512,128]{1,0:T(8,128)(2,1)S(1)}, u32[]{:S(2)}, u32[]{:S(2)}) collective-permute-start(bf16[512,128]{1,0:T(8,128)(2,1)S(1)} %bitcast.13), channel_id=1, source_target_pairs={{0,24},{8,16},{16,8},{24,0},{1,25},{9,17},{17,9},{25,1},{2,26},{10... | collective-permute-start | bytes 393224 | tf_op jit(solution)/shard_map/ppermute | solution.py:307
  34.0 5.9 %collective-permute-start.2 = (s32[32]{0:T(128)S(1)}, s32[32]{0:T(128)S(1)}, u32[]{:S(2)}, u32[]{:S(2)}) collective-permute-start(s32[32]{0:T(128)S(1)} %copy-done.2), channel_id=1, source_target_pairs={{0,1},{1,0},{2,3},{3,2},{4,5},{5,4},{6,7},{7,6},{8,9},{9,8},{10,11... | collective-permute-start | bytes 392 | tf_op jit(solution)/shard_map/ppermute | solution.py:310
